TPU v7x, 256 devices: a whole 4x4x8 slice. The times are simulated.
256 devices in a mesh: queue: 64 (over z, x, y_hi), shard: 4 (over y_lo, core).
Axes of the slice: x: 4, y: 4 (y_hi: 2, y_lo: 2; y = y_hi * 2 + y_lo), z: 8, core: 2. Of those that a mesh axis runs over, the one named last changes fastest.
Arguments:
- state: float32 [24576, 2560], P(('queue', 'shard')), may hold values from -150 to 150
- noise: bfloat16 [384, 2560], P('shard'), may hold values from -6 to 6
- modulation: bfloat16 [10, 3, 2560], replicated, may hold values from -3 to 3
- timesteps: int32 [64], P('queue'), may hold values from 0 to 9
- plan: float32 [11], replicated, may hold values from 0.02 to 1
- frame_ids: int32 [24576], replicated, may hold values from 0 to 511, never falling along the last dimension, each value on 1 to 96 neighbouring positions
- w_query: bfloat16 [2560, 2048], P(None, 'shard'), may hold values from -1 to 1
- w_key: bfloat16 [2560, 2048], P(None, 'shard'), may hold values from -40 to 40
- w_value: bfloat16 [2560, 2048], P(None, 'shard'), may hold values from -0.125 to 0.125
- w_out: bfloat16 [2048, 2560], P('shard'), may hold values from -0.125 to 0.125
Outputs:
- advanced: float32 [24576, 2560], P(('queue', 'shard'))
- estimate: bfloat16 [24576, 2560], P(('queue', 'shard'))
Inputs may be any that keep to these rules, and one draw needn't show every extreme that they name: `frame_ids`: frame numbers never fall along the tokens; each frame covers 1 to 96 consecutive tokens, and one frame exactly 96.
All inputs are finite; a program needn't handle non-finite values.
Results may differ from a plain program's by a relative error of at most 0.007.
Values may be sent and summed in bfloat16 or wider, within the bound.
A program may use at most 64 MiB of HBM per device.

v0:
```python
import math

import jax
import jax.numpy as jnp
from jax import lax
from jax.sharding import PartitionSpec as P

HEAD_DIM = 64


def extended(block, sides, width):
    for axis, dim in sides:
        count = lax.axis_size(axis)
        forward = [(i, i + 1) for i in range(count - 1)]
        backward = [(target, source) for source, target in forward]
        low = lax.ppermute(
            lax.slice_in_dim(block, block.shape[dim] - width, None, axis=dim), axis, forward
        )
        high = lax.ppermute(lax.slice_in_dim(block, 0, width, axis=dim), axis, backward)
        block = jnp.concatenate([low, block, high], axis=dim)
    return block


def from_behind(block, axis, distance):
    devices = range(lax.axis_size(axis))
    route = [(i - distance, i) for i in devices if i - distance in devices]
    return lax.ppermute(block, axis, route)


def normalize(hidden, modulate):
    center = jnp.mean(hidden, axis=-1, keepdims=True)
    spread = jnp.mean(jnp.square(hidden - center), axis=-1, keepdims=True)
    normed = (hidden - center) * lax.rsqrt(spread + 1e-06)
    return (normed * (1.0 + modulate[1]) + modulate[0]).astype(jnp.bfloat16)


def attend(queries, key_values, query_frames, key_frames):
    tok_slot = queries.shape[0]
    head_count = queries.shape[1] // HEAD_DIM
    query_heads = queries.reshape(tok_slot, head_count, HEAD_DIM)
    key_heads = key_values[:, 0].reshape(-1, head_count, HEAD_DIM)
    value_heads = key_values[:, 1].reshape(-1, head_count, HEAD_DIM)
    block_rows = min(512, tok_slot)
    block_count = tok_slot // block_rows
    score_scale = 1.0 / math.sqrt(HEAD_DIM)

    def one_block(block_index):
        scores = (
            jnp.einsum("qhd,khd->hqk", query_heads, key_heads, preferred_element_type=jnp.float32)
            * score_scale
        )
        allowed = jnp.abs(query_frames[:, None] - key_frames[None, :]) <= 1
        scores = jnp.where(allowed[None], scores, -1e30)
        row_max = jnp.max(scores, axis=-1, keepdims=True)
        weights = jnp.exp(scores - row_max)
        weights = (weights / jnp.sum(weights, axis=-1, keepdims=True)).astype(jnp.bfloat16)
        mixed = jnp.einsum("hqk,khd->qhd", weights, value_heads, preferred_element_type=jnp.float32)
        return mixed.astype(jnp.bfloat16).reshape(block_rows, head_count * HEAD_DIM)

    blocks = lax.map(one_block, jnp.arange(block_count, dtype=jnp.int32))
    return blocks.reshape(tok_slot, head_count * HEAD_DIM)


def on_device(state, noise, modulation, timesteps, plan, frame_ids, w_query, w_key, w_value, w_out):
    shard_count = lax.axis_size("shard")
    slot_index = lax.axis_index("queue")
    tok_dev = state.shape[0]
    tok_slot = tok_dev * shard_count
    noise_level = timesteps[0]
    modulate = lax.dynamic_index_in_dim(modulation, noise_level, 0, keepdims=False).astype(
        jnp.float32
    )
    normed = normalize(state, modulate)
    shard_rows = lax.all_gather(normed, "shard", axis=0, tiled=True)
    projected = jnp.stack(
        [
            jnp.dot(shard_rows, w_query, preferred_element_type=jnp.float32),
            jnp.dot(shard_rows, w_key, preferred_element_type=jnp.float32),
            jnp.dot(shard_rows, w_value, preferred_element_type=jnp.float32),
        ],
        axis=1,
    ).astype(jnp.bfloat16)
    queries = projected[:, 0]
    key_values = projected[:, 1:]
    beside_all = extended(key_values, (("queue", 0),), tok_slot)
    padded_frames = jnp.pad(frame_ids, (tok_slot, tok_slot), constant_values=-(1 << 20))
    slot_start = slot_index * tok_slot
    key_frames = lax.dynamic_slice_in_dim(padded_frames, slot_start, tok_slot + 2 * tok_slot, 0)
    query_frames = lax.dynamic_slice_in_dim(frame_ids, slot_start, tok_slot, 0)
    attended = attend(queries, beside_all, query_frames, key_frames)
    attn_sum = lax.psum_scatter(
        jnp.dot(attended, w_out, preferred_element_type=jnp.float32).astype(jnp.bfloat16),
        "shard",
        scatter_dimension=0,
        tiled=True,
    ).astype(jnp.float32)
    velocity = modulate[2] * attn_sum
    sigma_now = plan[noise_level]
    sigma_next = plan[noise_level + 1]
    estimate = (state - sigma_now * velocity).astype(jnp.bfloat16)
    moved = state + (sigma_next - sigma_now) * velocity
    shifted = from_behind(moved.astype(jnp.bfloat16), "queue", 1).astype(moved.dtype)
    advanced = jnp.where(slot_index == 0, noise.astype(jnp.float32), shifted)
    return (advanced, estimate)


def solution(mesh):
    return jax.shard_map(
        on_device,
        mesh=mesh,
        in_specs=(
            P(("queue", "shard"), None),
            P("shard", None),
            P(),
            P("queue"),
            P(),
            P(),
            P(None, "shard"),
            P(None, "shard"),
            P(None, "shard"),
            P("shard", None),
        ),
        out_specs=(P(("queue", "shard"), None), P(("queue", "shard"), None)),
        check_vma=False,
    )
```

profile of v0, /device:TPU:129, one launch (start us, length us, event | category | flops | bytes accessed | tf_op | source)
XLA Modules:
  0.0 182.0 jit_solution(17102279058636200222)
XLA Ops:
  8.0 1.3 reduce_sum.28
  9.4 1.5 multiply_reduce_fusion
  10.9 0.7 dynamic-slice_convert_fusion
  11.6 0.1 slice_reduce_fusion.1
  11.7 2.2 %add_convert_fusion.1 = bf16[96,2560]{1,0:T(8,128)(2,1)} fusion(f32[96,2560]{1,0:T(8,128)} %param.10, f32[2560]{0:T(1024)S(1)} %get-tuple-element.17, f32[2560]{0:T(1024)S(1)} %get-tuple-element.18, f32[96]{0:T(128)S(1)} %add_rsqrt_fusion, f32[96]{0:T(128)S(1)} %broadcast_multiply_fusion), kind=kLoop, calls=%fused_computation.23 | loop fusion | flops 1228800 | bytes 1495808 | tf_op jit(solution)/shard_map/convert_element_type | solution.py:34
  14.0 0.0 reduce-scatter.2.cloned.1.call-start
  14.0 0.1 dynamic_slice.19
  14.1 0.1 pad_dynamic-slice_fusion
  14.2 32.5 %all-gather.2.cloned.1.call-done = bf16[384,2560]{1,0:T(8,128)(2,1)} async-done(((bf16[96,2560]{1,0:T(8,128)(2,1)}), bf16[384,2560]{1,0:T(8,128)(2,1)}) %all-gather.2.cloned.1.call-update) | async-done | bytes 1966096 | tf_op jit(solution)/shard_map/all_gather | solution.py:74
  46.6 3.7 %fusion.10 = bf16[384,1,512]{2,0,1:T(8,128)(2,1)S(1)} fusion(bf16[384,2560]{1,0:T(8,128)(2,1)} %all-gather.2.cloned.1.call-done, bf16[2560,512]{1,0:T(8,128)(2,1)} %param.18), kind=kOutput, calls=%fused_computation.18 | convolution fusion | flops 1006829568 | bytes 4980736 | tf_op jit(solution)/shard_map/dot_general | solution.py:79
  50.4 1.2 fusion.9
  51.5 0.9 pad_maximum_fusion.1
  52.5 6.4 %collective-permute-start.1 = (bf16[384,2,512]{2,0,1:T(8,128)(2,1)}, bf16[384,2,512]{2,0,1:T(8,128)(2,1)}, u32[]{:S(2)}, u32[]{:S(2)}) collective-permute-start(bf16[384,2,512]{2,0,1:T(8,128)(2,1)} %pad_maximum_fusion.1), channel_id=1, source_target_pairs={{4,0},{8,4},{12,8},{16,12},{20,16},{24,20},{28,24},{32,28},{36,32}... | collective-permute-start | bytes 2359304 | tf_op jit(solution)/shard_map/ppermute | solution.py:19
  58.9 1.9 %collective-permute-start = (bf16[384,2,512]{2,0,1:T(8,128)(2,1)}, bf16[384,2,512]{2,0,1:T(8,128)(2,1)}, u32[]{:S(2)}, u32[]{:S(2)}) collective-permute-start(bf16[384,2,512]{2,0,1:T(8,128)(2,1)} %pad_maximum_fusion.1), channel_id=1, source_target_pairs={{0,4},{4,8},{8,12},{12,16},{16,20},{20,24},{24,28},{28,32},{32,36}... | collective-permute-start | bytes 2359304 | tf_op jit(solution)/shard_map/ppermute | solution.py:16
  60.8 1.3 abs_compare_fusion
  62.1 1.9 %convolution_convert_fusion.1 = bf16[384,512]{1,0:T(8,128)(2,1)} fusion(bf16[384,2560]{1,0:T(8,128)(2,1)S(1)} %copy-done.8, bf16[2560,512]{1,0:T(8,128)(2,1)S(1)} %copy-done.7), kind=kOutput, calls=%fused_computation.13 | convolution fusion | flops 1006829568 | bytes 4980736 | tf_op jit(solution)/shard_map/dot_general | solution.py:77
  64.0 1.9 %copy.16 = bf16[384,512]{0,1:T(8,128)(2,1)} copy(bf16[384,512]{1,0:T(8,128)(2,1)} %convolution_convert_fusion.1) | data formatting | bytes 786432 | tf_op jit(solution)/shard_map/convert.5
  65.9 26.1 %collective-permute-done.1 = bf16[384,2,512]{2,0,1:T(8,128)(2,1)} collective-permute-done((bf16[384,2,512]{2,0,1:T(8,128)(2,1)}, bf16[384,2,512]{2,0,1:T(8,128)(2,1)}, u32[]{:S(2)}, u32[]{:S(2)}) %collective-permute-start.1) | collective-permute-done | bytes 786464 | tf_op jit(solution)/shard_map/ppermute | solution.py:19
  92.1 0.2 collective-permute-done
  92.2 1.5 pad_maximum_fusion
  93.7 1.6 fusion.19
  95.3 2.4 %copy.17 = bf16[1152,1,512]{0,2,1:T(8,128)(2,1)} copy(bf16[1152,1,512]{2,0,1:T(8,128)(2,1)} %get-tuple-element.19) | data formatting | bytes 2359296 | tf_op jit(solution)/shard_map/slice | solution.py:41
  97.8 2.4 %copy.15 = bf16[1152,1,512]{0,2,1:T(8,128)(2,1)} copy(bf16[1152,1,512]{2,0,1:T(8,128)(2,1)} %get-tuple-element.20) | data formatting | bytes 2359296 | tf_op jit(solution)/shard_map/slice | solution.py:42
  100.1 6.1 %fusion.21 = f32[8,384]{1,0:T(8,128)S(1)} fusion(pred[384,1152]{1,0:T(8,128)(4,1)S(1)} %copy-done.2, bf16[384,8,64]{0,2,1:T(8,128)(2,1)S(1)} %bitcast.38, bf16[1152,8,64]{0,2,1:T(8,128)(2,1)} %bitcast.33), kind=kOutput, calls=%fused_computation.41 | convolution fusion | flops 467141760 | bytes 2027520 | tf_op jit(solution)/shard_map/while/body/eval_jaxpr/sub | solution.py:55
  106.2 7.5 %fusion.8 = bf16[8,64,384]{2,1,0:T(8,128)(2,1)S(1)} fusion(bf16[1152,8,64]{0,2,1:T(8,128)(2,1)} %bitcast.35, f32[8,384]{1,0:T(8,128)S(1)} %fusion.21, pred[384,1152]{1,0:T(8,128)(4,1)S(1)} %copy-done.2, bf16[384,8,64]{0,2,1:T(8,128)(2,1)} %bitcast.37, bf16[1152,8,64]{0,2,1:T(8,128)(2,1)} %bitcast.34), kind=kOutput, calls=%fused_computation.16 | convolution fusion | flops 923865216 | bytes 3600384 | tf_op jit(solution)/shard_map/while/body/eval_jaxpr/hqk,khd->qhd/dot_general | solution.py:57
  113.7 2.5 %convolution_convert_fusion = bf16[384,2560]{1,0:T(8,128)(2,1)} fusion(bf16[384,512]{0,1:T(8,128)(2,1)S(1)} %bitcast.36, bf16[512,2560]{1,0:T(8,128)(2,1)S(1)} %copy-done), kind=kOutput, calls=%fused_computation.9 | convolution fusion | flops 1007616000 | bytes 4980736 | tf_op jit(solution)/shard_map/dot_general | solution.py:92
  116.3 0.7 fusion.20
  118.2 31.5 %reduce-scatter.2.cloned.1.call-done = bf16[96,2560]{1,0:T(8,128)(2,1)} async-done(((bf16[384,2560]{1,0:T(8,128)(2,1)}), bf16[96,2560]{1,0:T(8,128)(2,1)}) %reduce-scatter.2.cloned.1.call-update) | async-done | bytes 491536 | tf_op jit(solution)/shard_map/reduce_scatter | solution.py:91
  149.7 3.1 %subtract_convert_fusion = (bf16[96,2560]{1,0:T(8,128)(2,1)}, bf16[96,2560]{1,0:T(8,128)(2,1)}) fusion(f32[96,2560]{1,0:T(8,128)} %param.10, bf16[96,2560]{1,0:T(8,128)(2,1)} %reduce-scatter.2.cloned.1.call-done, f32[]{:T(128)} %bitcast.2, f32[2560]{0:T(1024)S(1)} %get-tuple-element.16, f32[]{:T(128)S(6)} %sub.54), kind=kLoop, calls=%fused_computation.19 | loop fusion | flops 1966080 | bytes 2467848 | tf_op jit(solution)/shard_map/convert_element_type | solution.py:100
  152.8 4.3 %collective-permute-start.2 = (bf16[96,2560]{1,0:T(8,128)(2,1)}, bf16[96,2560]{1,0:T(8,128)(2,1)}, u32[]{:S(2)}, u32[]{:S(2)}) collective-permute-start(bf16[96,2560]{1,0:T(8,128)(2,1)} %get-tuple-element.29), channel_id=1, source_target_pairs={{0,4},{4,8},{8,12},{12,16},{16,20},{20,24},{24,28},{28,32},{32,36}... | collective-permute-start | bytes 1474568 | tf_op jit(solution)/shard_map/ppermute | solution.py:27
  157.1 16.0 %collective-permute-done.2 = bf16[96,2560]{1,0:T(8,128)(2,1)} collective-permute-done((bf16[96,2560]{1,0:T(8,128)(2,1)}, bf16[96,2560]{1,0:T(8,128)(2,1)}, u32[]{:S(2)}, u32[]{:S(2)}) %collective-permute-start.2) | collective-permute-done | bytes 491552 | tf_op jit(solution)/shard_map/ppermute | solution.py:27
  173.1 2.1 %convert_select_fusion = f32[96,2560]{1,0:T(8,128)} fusion(bf16[96,2560]{1,0:T(8,128)(2,1)} %collective-permute-done.2, bf16[96,2560]{1,0:T(8,128)(2,1)S(1)} %copy-done.1, pred[]{:T(512)S(6)} %eq.3), kind=kLoop, calls=%fused_computation.20 | loop fusion | flops 737280 | bytes 1966081 | tf_op jit(solution)/shard_map/jit(_where)/select_n | solution.py:103
  (23 shorter events, 0.2 us)
Async XLA Ops:
  7.2 106.6 %copy-start = (bf16[512,2560]{1,0:T(8,128)(2,1)S(1)}, bf16[512,2560]{1,0:T(8,128)(2,1)}, u32[]{:S(2)}) copy-start(bf16[512,2560]{1,0:T(8,128)(2,1)} %param.19) | copy-start | bytes 7864324
  7.2 6.8 %copy-start.4 = (s32[24576]{0:T(1024)S(1)}, s32[24576]{0:T(1024)}, u32[]{:S(2)}) copy-start(s32[24576]{0:T(1024)} %param.15) | copy-start | bytes 294916
  7.2 39.5 %all-gather.2.cloned.1.call-start = ((), (), s32[]{:S(2)}) async-start(), calls=%async_computation.1 | async-start | bytes 2457600 | tf_op jit(solution)/shard_map/all_gather | solution.py:74
  14.0 135.7 %reduce-scatter.2.cloned.1.call-start = ((), (), s32[]{:S(2)}) async-start(), calls=%async_computation.2 | async-start | bytes 2457600 | tf_op jit(solution)/shard_map/reduce_scatter | solution.py:91
  46.6 3.7 %copy-start.6 = (bf16[2560,512]{1,0:T(8,128)(2,1)S(1)}, bf16[2560,512]{1,0:T(8,128)(2,1)}, u32[]{:S(2)}) copy-start(bf16[2560,512]{1,0:T(8,128)(2,1)} %param.17) | copy-start | bytes 7864324
  46.6 3.7 %copy-start.8 = (bf16[384,2560]{1,0:T(8,128)(2,1)S(1)}, bf16[384,2560]{1,0:T(8,128)(2,1)}, u32[]{:S(2)}) copy-start(bf16[384,2560]{1,0:T(8,128)(2,1)} %all-gather.2.cloned.1.call-done) | copy-start | bytes 5898244
  50.4 11.7 %copy-start.7 = (bf16[2560,512]{1,0:T(8,128)(2,1)S(1)}, bf16[2560,512]{1,0:T(8,128)(2,1)}, u32[]{:S(2)}) copy-start(bf16[2560,512]{1,0:T(8,128)(2,1)} %param.16) | copy-start | bytes 7864324
  52.5 39.6 %collective-permute-start.1 = (bf16[384,2,512]{2,0,1:T(8,128)(2,1)}, bf16[384,2,512]{2,0,1:T(8,128)(2,1)}, u32[]{:S(2)}, u32[]{:S(2)}) collective-permute-start(bf16[384,2,512]{2,0,1:T(8,128)(2,1)} %pad_maximum_fusion.1), channel_id=1, source_target_pairs={{4,0},{8,4},{12,8},{16,12},{20,16},{24,20},{28,24},{32,28},{36,32}... | collective-permute-start | bytes 2359304 | tf_op jit(solution)/shard_map/ppermute | solution.py:19
  58.9 33.3 %collective-permute-start = (bf16[384,2,512]{2,0,1:T(8,128)(2,1)}, bf16[384,2,512]{2,0,1:T(8,128)(2,1)}, u32[]{:S(2)}, u32[]{:S(2)}) collective-permute-start(bf16[384,2,512]{2,0,1:T(8,128)(2,1)} %pad_maximum_fusion.1), channel_id=1, source_target_pairs={{0,4},{4,8},{8,12},{12,16},{16,20},{20,24},{24,28},{28,32},{32,36}... | collective-permute-start | bytes 2359304 | tf_op jit(solution)/shard_map/ppermute | solution.py:16
  95.3 4.8 %copy-start.2 = (pred[384,1152]{1,0:T(8,128)(4,1)S(1)}, pred[384,1152]{1,0:T(8,128)(4,1)}, u32[]{:S(2)}) copy-start(pred[384,1152]{1,0:T(8,128)(4,1)} %abs_compare_fusion) | copy-start | bytes 1327108
  95.3 4.8 %copy-start.3 = (bf16[384,512]{0,1:T(8,128)(2,1)S(1)}, bf16[384,512]{0,1:T(8,128)(2,1)}, u32[]{:S(2)}) copy-start(bf16[384,512]{0,1:T(8,128)(2,1)} %copy.16) | copy-start | bytes 1179652
  113.7 2.5 %copy-start.5 = (f32[11]{0:T(128)S(1)}, f32[11]{0:T(128)}, u32[]{:S(2)}) copy-start(f32[11]{0:T(128)} %param.14) | copy-start | bytes 136
  116.2 56.9 %copy-start.1 = (bf16[96,2560]{1,0:T(8,128)(2,1)S(1)}, bf16[96,2560]{1,0:T(8,128)(2,1)}, u32[]{:S(2)}) copy-start(bf16[96,2560]{1,0:T(8,128)(2,1)} %param.11) | copy-start | bytes 1474564
  152.8 20.3 %collective-permute-start.2 = (bf16[96,2560]{1,0:T(8,128)(2,1)}, bf16[96,2560]{1,0:T(8,128)(2,1)}, u32[]{:S(2)}, u32[]{:S(2)}) collective-permute-start(bf16[96,2560]{1,0:T(8,128)(2,1)} %get-tuple-element.29), channel_id=1, source_target_pairs={{0,4},{4,8},{8,12},{12,16},{16,20},{20,24},{24,28},{28,32},{32,36}... | collective-permute-start | bytes 1474568 | tf_op jit(solution)/shard_map/ppermute | solution.py:27
Sparse Core Ops, SparseCore 0:
  14.1 32.5 all-gather.1
  116.4 33.2 reduce-scatter.1
where the time goes:
time: 183 us; the launch traced here: 182 us
  waiting for transfers between devices  106 us (58%)
  matrix products  22.8 us (12%)
  between operations  16.3 us (9%)
  other arithmetic  14.8 us (8%)
  starting transfers between devices  12.7 us (7%)
  local copies, waits for them, and re-layouts  9.18 us (5%)
    all_gather x1, waiting for transfers between devices, on_device(): shard_rows = lax.all_gather(normed, 'shard', axis=0, tiled=True)  32.5 us
    reduce_scatter x1, waiting for transfers between devices, on_device(): lax.psum_scatter(jnp.dot(attended, w_out, preferred_element_type=jnp.floa...  31.5 us
    ppermute x1, waiting for transfers between devices, extended(): lax.ppermute(lax.slice_in_dim(block, 0, width, axis=dim), axis, backward)  26.1 us
    ppermute x1, waiting for transfers between devices, from_behind(): return lax.ppermute(block, axis, route)  16 us
    dot_general x1, matrix products, one_block(): jnp.einsum('hqk,khd->qhd', weights, value_heads, preferred_element_type=j...  7.53 us
    ppermute x1, starting transfers between devices, extended(): lax.ppermute(lax.slice_in_dim(block, 0, width, axis=dim), axis, backward)  6.37 us
    sub x1, matrix products, one_block(): weights = jnp.exp(scores - row_max)  6.05 us
    ppermute x1, starting transfers between devices, from_behind(): return lax.ppermute(block, axis, route)  4.35 us
  transfers between devices with their start and end apart: 5, of which 5 were waited for; matrix products, arithmetic and copies ran while one was open for 3% of the time, Pallas kernels for 0%

commit v1 on v0

v1 whole, which is shorter than its diff:
```python
import functools

import jax
import jax.numpy as jnp
from jax import lax
from jax.experimental import pallas as pl
from jax.experimental.pallas import tpu as pltpu
from jax.sharding import PartitionSpec as P

MESH = pl.DeviceIdType.MESH
ROWS = 96
HALF = 48
BF16 = jnp.bfloat16
F32 = jnp.float32


def kernel(
    state_h, noise_h, mod_ref, step_ref, plan_ref, frame_ref, wq_h, wk_h, wv_h, wo_h,
    adv_h, est_h,
    state, noise, blocks, w_in, w_out, queries, kv, bias, mixed, mixed_sib,
    own_sum, far_sum, far_in, moved, moved_in, adv, est,
    load_sem, store_sem, send_sem, recv_sem, pair_send, pair_recv,
    far_send, far_recv, move_send, move_recv,
):
    width = state.shape[1]
    inner = queries.shape[1]
    chunks, _, span = own_sum.shape
    pairs = inner // 128
    slots = lax.axis_size("queue")
    slot = lax.axis_index("queue")
    shard = lax.axis_index("shard")
    side = lax.div(shard, 2)
    core = lax.rem(shard, 2)
    other = 1 - core
    chain = 2 * slots
    chip = 2 * slot + side

    def at(step, which):
        there = lax.rem(chip + step + chain, chain)
        return (lax.div(there, 2), 2 * lax.rem(there, 2) + which)

    sibling = (slot, 2 * side + other)
    ahead = at(1, core)
    behind = at(-1, core)
    across = at(2 * core - 1, other)

    barrier = pltpu.get_barrier_semaphore()
    for device in (sibling, ahead, behind, across, at(-2, core)):
        pl.semaphore_signal(barrier, inc=1, device_id=device, device_id_type=MESH)

    def load(source, target, n):
        copy = pltpu.make_async_copy(source, target, load_sem.at[n])
        copy.start()
        return copy

    load_state = load(state_h, state, 0)
    load_w = [
        load(w, w_in.at[:, pl.ds(n * inner, inner)], 1 + n)
        for n, w in enumerate((wq_h, wk_h, wv_h))
    ]
    load_wo = load(wo_h, w_out.at[0], 4)
    load_noise = load(noise_h, noise, 5)

    level = step_ref[0]
    modulate = mod_ref[level].astype(F32)
    shift, gain, gate = modulate[0:1], 1.0 + modulate[1:2], modulate[2:3]
    sigma_now = plan_ref[level]
    sigma_step = plan_ref[level + 1] - sigma_now
    mine = blocks.at[4 + core]
    load_state.wait()

    def normalise(n, _):
        rows = pl.ds(pl.multiple_of(n * 16, 16), 16)
        x = state[rows, :]
        x = x - jnp.mean(x, axis=-1, keepdims=True)
        spread = jnp.mean(jnp.square(x), axis=-1, keepdims=True)
        blocks[4 + core, rows, :] = (x * lax.rsqrt(spread + 1e-06) * gain + shift).astype(BF16)
        return 0

    lax.fori_loop(0, ROWS // 16, normalise, 0)
    pl.semaphore_wait(barrier, 5)

    sends = []

    def send(place, half, to_place, device, n):
        rows = pl.ds(half * HALF, HALF)
        copy = pltpu.make_async_remote_copy(
            src_ref=blocks.at[place, rows],
            dst_ref=blocks.at[to_place, rows],
            send_sem=send_sem.at[n],
            recv_sem=recv_sem.at[to_place, half],
            device_id=device,
            device_id_type=MESH,
        )
        return copy

    def wait_block(place, half):
        rows = pl.ds(half * HALF, HALF)
        here = blocks.at[place, rows]
        pltpu.make_async_copy(here, here, recv_sem.at[place, half]).wait()

    for half in range(2):
        sends.append(send(4 + core, half, 2 + core, ahead, 3 * half))
        sends.append(send(4 + core, half, 6 + core, behind, 3 * half + 1))
        sends.append(send(4 + core, half, 4 + core, sibling, 3 * half + 2))
    for copy in sends:
        copy.start()
    share_w = pltpu.make_async_remote_copy(
        src_ref=wo_h, dst_ref=w_out.at[1], send_sem=pair_send.at[0], recv_sem=pair_recv.at[0],
        device_id=sibling, device_id_type=MESH,
    )
    share_w.start()

    first = 192 * chip - 288 + chain * 192
    row = lax.div(first, 128)
    lines = [
        frame_ref[pl.ds(lax.rem(row + n, chain * 192 // 128), 1), :] for n in range(7)
    ]
    line = jnp.concatenate(lines, axis=1).astype(F32)
    line = jnp.broadcast_to(line, (8, 896))
    line = jnp.where(side == 0, pltpu.roll(line, 896 - 96, 1), pltpu.roll(line, 896 - 32, 1))
    column = jnp.broadcast_to(pltpu.roll(line, 896 - 192, 1)[0:1, :384], (128, 384)).T
    for n in range(4):
        keys = line if n == 0 else pltpu.roll(line, 896 - 96 * n, 1)
        gap = jnp.abs(column[n * ROWS:(n + 1) * ROWS, 0:1] - keys[0:1, :512])
        bias[n] = jnp.where(gap <= 1.0, 0.0, -1e30)
    kv[pl.ds(8 * ROWS, 32), :] = jnp.zeros((32, 2 * inner), BF16)

    def project(place, count, col, target, target_row):
        def part(n, _):
            into = pl.multiple_of(n * 256, 256)
            x = blocks[pl.ds(place, count)].reshape(count * ROWS, width)
            y = jnp.dot(x, w_in[:, pl.ds(col + into, 256)], preferred_element_type=F32)
            target[pl.ds(target_row, count * ROWS), pl.ds(into, 256)] = y.astype(BF16)
            return 0
        return part

    def project_q(place, count, row_):
        def part(n, _):
            into = pl.multiple_of(n * 256, 256)
            x = blocks[place:place + count].reshape(count * ROWS, width)
            y = jnp.dot(x, w_in[:, pl.ds(into, 256)], preferred_element_type=F32)
            queries[pl.ds(row_, count * ROWS), pl.ds(into, 256)] = y.astype(BF16) * 0.125
            return 0
        lax.fori_loop(0, inner // 256, part, 0)

    def project_kv(place, rows_):
        def part(n, _):
            into = pl.multiple_of(n * 256, 256)
            x = blocks[place:place + 2].reshape(2 * ROWS, width)
            w = w_in[:, pl.ds(pl.multiple_of(inner + into, 256), 256)]
            y = jnp.dot(x, w, preferred_element_type=F32).astype(BF16)
            for k, row_ in enumerate(rows_):
                kv[pl.ds(row_, ROWS), pl.ds(into, 256)] = y[k * ROWS:(k + 1) * ROWS]
            return 0
        lax.fori_loop(0, 2 * inner // 256, part, 0)

    def attend(n):
        lane = lax.broadcasted_iota(jnp.int32, (ROWS, 128), 1)
        low = lane < 64

        def pair(g, _):
            cols = pl.ds(pl.multiple_of(g * 128, 128), 128)
            v_cols = pl.ds(pl.multiple_of(inner + g * 128, 128), 128)
            q = queries[pl.ds(n * ROWS, ROWS), cols]
            zero = jnp.zeros_like(q)
            q = jnp.concatenate([jnp.where(low, q, zero), jnp.where(low, zero, q)], axis=0)
            k = kv[pl.ds(n * ROWS, 512), cols]
            v = kv[pl.ds(n * ROWS, 512), v_cols]
            s = lax.dot_general(q, k, (((1,), (1,)), ((), ())), preferred_element_type=F32)
            s = s + jnp.concatenate([bias[n], bias[n]], axis=0)
            w = jnp.exp(s - jnp.max(s, axis=-1, keepdims=True))
            total = jnp.sum(w, axis=-1, keepdims=True)
            o = jnp.dot(w.astype(BF16), v, preferred_element_type=F32) / total
            mixed[n, :, cols] = jnp.where(low, o[:ROWS], o[ROWS:]).astype(BF16)
            return 0
        lax.fori_loop(0, pairs, pair, 0)

    for half in range(2):
        wait_block(4 + other, half)
    for copy in load_w:
        copy.wait()
    project_q(4, 2, ROWS)
    project_kv(4, (3 * ROWS, 4 * ROWS))

    def forward(place, half, n):
        wait_block(place, half)
        send(place, half, place, sibling, n).start()

    def relay_ahead():
        rows = pl.ds(pl.multiple_of(core * HALF, 16), HALF)
        return pltpu.make_async_remote_copy(
            src_ref=blocks.at[3, rows], dst_ref=blocks.at[1, rows],
            send_sem=send_sem.at[10], recv_sem=recv_sem.at[1, core],
            device_id=ahead, device_id_type=MESH,
        )

    def relay_behind():
        rows = pl.ds(pl.multiple_of(core * HALF, 16), HALF)
        return pltpu.make_async_remote_copy(
            src_ref=blocks.at[6, rows], dst_ref=blocks.at[0, rows],
            send_sem=send_sem.at[11], recv_sem=recv_sem.at[0, core],
            device_id=behind, device_id_type=MESH,
        )

    @pl.when(core == 0)
    def _():
        forward(2, 0, 6)
        forward(6, 0, 7)
        relay_behind().start()
        wait_block(3, 0)
        relay_ahead().start()
        forward(2, 1, 8)
        forward(6, 1, 9)
        wait_block(3, 1)
        wait_block(7, 0)
        wait_block(7, 1)

    @pl.when(core == 1)
    def _():
        forward(3, 0, 6)
        forward(7, 0, 7)
        forward(3, 1, 8)
        relay_ahead().start()
        forward(7, 1, 9)
        wait_block(6, 0)
        wait_block(6, 1)
        relay_behind().start()
        wait_block(2, 0)
        wait_block(2, 1)

    project_q(3, 1, 0)
    project_q(6, 1, 3 * ROWS)
    project_kv(2, (ROWS, 2 * ROWS))
    project_kv(6, (5 * ROWS, 6 * ROWS))
    attend(1)
    attend(2)

    for k in range(2):
        rows = pl.ds(pl.multiple_of(core * HALF, 16), HALF)
        here = blocks.at[k, rows]
        pltpu.make_async_copy(here, here, recv_sem.at[k, core]).wait()
        pltpu.make_async_remote_copy(
            src_ref=here, dst_ref=here, send_sem=send_sem.at[12 + k],
            recv_sem=recv_sem.at[k, core], device_id=sibling, device_id_type=MESH,
        ).start()
    for k in range(2):
        rows = pl.ds(pl.multiple_of(other * HALF, 16), HALF)
        here = blocks.at[k, rows]
        pltpu.make_async_copy(here, here, recv_sem.at[k, other]).wait()
    project_kv(0, (7 * ROWS, 0))
    attend(0)
    attend(3)

    theirs = pl.ds(pl.multiple_of(other * HALF, 16), HALF)
    ours = pl.ds(pl.multiple_of(core * HALF, 16), HALF)
    swaps = []
    for n, (source, start, count) in enumerate((
        (mixed.at[0, theirs], 0, HALF),
        (mixed.at[3, theirs], HALF, HALF),
        (mixed.at[1 + other], ROWS, ROWS),
    )):
        swaps.append(pltpu.make_async_remote_copy(
            src_ref=source, dst_ref=mixed_sib.at[pl.ds(start, count)],
            send_sem=pair_send.at[1 + n], recv_sem=pair_recv.at[1 + n],
            device_id=sibling, device_id_type=MESH,
        ))
    for copy in swaps:
        copy.start()
    load_wo.wait()
    share_w.wait()
    for copy in swaps:
        copy.wait()

    far = []
    far_mine = jnp.concatenate([mixed[0, ours, :], mixed[3, ours, :]], axis=0)
    for n in range(chunks):
        cols = pl.ds(n * span, span)
        y = jnp.dot(far_mine, w_out[0, :, cols], preferred_element_type=F32)
        y += jnp.dot(mixed_sib[0:ROWS], w_out[1, :, cols], preferred_element_type=F32)
        far_sum[n] = y.astype(BF16)
        for k, device in enumerate((at(-1, 1), at(1, 0))):
            copy = pltpu.make_async_remote_copy(
                src_ref=far_sum.at[n, pl.ds(k * HALF, HALF)],
                dst_ref=far_in.at[n, ours],
                send_sem=far_send.at[n, k], recv_sem=far_recv.at[n, core],
                device_id=device, device_id_type=MESH,
            )
            copy.start()
            far.append(copy)
    for n in range(chunks):
        cols = pl.ds(n * span, span)
        y = jnp.dot(mixed[1 + core], w_out[0, :, cols], preferred_element_type=F32)
        y += jnp.dot(mixed_sib[ROWS:2 * ROWS], w_out[1, :, cols], preferred_element_type=F32)
        own_sum[n] = y
    moves = []
    for n in range(chunks):
        for k in range(2):
            here = far_in.at[n, pl.ds(k * HALF, HALF)]
            pltpu.make_async_copy(here, here, far_recv.at[n, k]).wait()
        cols = slice(n * span, (n + 1) * span)
        velocity = gate[:, cols] * (own_sum[n] + far_in[n].astype(F32))
        x = state[:, cols]
        moved[n] = (x + sigma_step * velocity).astype(BF16)
        copy = pltpu.make_async_remote_copy(
            src_ref=moved.at[n], dst_ref=moved_in.at[n],
            send_sem=move_send.at[n], recv_sem=move_recv.at[n],
            device_id=at(2, core), device_id_type=MESH,
        )
        copy.start()
        moves.append(copy)
        est[:, cols] = (x - sigma_now * velocity).astype(BF16)
    store_est = pltpu.make_async_copy(est, est_h, store_sem.at[0])
    store_est.start()
    load_noise.wait()
    stores = []
    for n in range(chunks):
        moves[n].wait()
        cols = slice(n * span, (n + 1) * span)
        adv[:, cols] = jnp.where(slot == 0, noise[:, cols].astype(F32), moved_in[n].astype(F32))
        copy = pltpu.make_async_copy(
            adv.at[:, pl.ds(n * span, span)], adv_h.at[:, pl.ds(n * span, span)], store_sem.at[1 + n]
        )
        copy.start()
        stores.append(copy)

    for copy in sends:
        copy.wait_send()
    for n in range(6, 14):
        here = blocks.at[0, pl.ds(0, HALF)]
        pltpu.make_async_copy(here, here, send_sem.at[n]).wait()
    for copy in far:
        copy.wait_send()
    store_est.wait()
    for copy in stores:
        copy.wait()


def on_device(state, noise, modulation, timesteps, plan, frame_ids, w_query, w_key, w_value, w_out):
    rows, width = state.shape
    inner = w_query.shape[1]
    span = 512
    chunks = width // span
    hbm = pl.BlockSpec(memory_space=pl.ANY)
    vmem = pl.BlockSpec(memory_space=pltpu.VMEM)
    smem = pl.BlockSpec(memory_space=pltpu.SMEM)
    dma = pltpu.SemaphoreType.DMA
    advanced, estimate = pl.pallas_call(
        kernel,
        out_shape=(
            jax.ShapeDtypeStruct((rows, width), F32),
            jax.ShapeDtypeStruct((rows, width), BF16),
        ),
        in_specs=[hbm, hbm, vmem, smem, smem, vmem, hbm, hbm, hbm, hbm],
        out_specs=(hbm, hbm),
        scratch_shapes=[
            pltpu.VMEM((rows, width), F32),
            pltpu.VMEM((rows, width), BF16),
            pltpu.VMEM((8, rows, width), BF16),
            pltpu.VMEM((width, 3 * inner), BF16),
            pltpu.VMEM((2, inner, width), BF16),
            pltpu.VMEM((4 * rows, inner), BF16),
            pltpu.VMEM((8 * rows + 32, 2 * inner), BF16),
            pltpu.VMEM((4, rows, 512), F32),
            pltpu.VMEM((4, rows, inner), BF16),
            pltpu.VMEM((2 * rows, inner), BF16),
            pltpu.VMEM((chunks, rows, span), F32),
            pltpu.VMEM((chunks, rows, span), BF16),
            pltpu.VMEM((chunks, rows, span), BF16),
            pltpu.VMEM((chunks, rows, span), BF16),
            pltpu.VMEM((chunks, rows, span), BF16),
            pltpu.VMEM((rows, width), F32),
            pltpu.VMEM((rows, width), BF16),
            dma((6,)),
            dma((1 + chunks,)),
            dma((14,)),
            dma((8, 2)),
            dma((4,)),
            dma((4,)),
            dma((chunks, 2)),
            dma((chunks, 2)),
            dma((chunks,)),
            dma((chunks,)),
        ],
        compiler_params=pltpu.CompilerParams(
            collective_id=0, has_side_effects=True, vmem_limit_bytes=48 << 20
        ),
        name="step",
    )(
        state, noise, modulation, timesteps, plan, frame_ids.reshape(-1, 128),
        w_query, w_key, w_value, w_out,
    )
    return advanced, estimate


def solution(mesh):
    return jax.shard_map(
        on_device,
        mesh=mesh,
        in_specs=(
            P(("queue", "shard"), None),
            P("shard", None),
            P(),
            P("queue"),
            P(),
            P(),
            P(None, "shard"),
            P(None, "shard"),
            P(None, "shard"),
            P("shard", None),
        ),
        out_specs=(P(("queue", "shard"), None), P(("queue", "shard"), None)),
        check_vma=False,
    )
```

time: 183 us -> 79.5 us (0.43)
  the two profiles are of different devices: /device:TPU:129 before, /device:TPU:1 now
where the time goes in v1:
time: 79.5 us; the launch traced here: 79.2 us
  Pallas kernels  69.7 us (88%)
  local copies, waits for them, and re-layouts  8.16 us (10%)
  between operations  1.3 us (2%)
    pallas_call x1, Pallas kernels, on_device(): pl.pallas_call(kernel, out_shape=(jax.ShapeDtypeStruct((rows, width), F32...  69.7 us
    unnamed x14, local copies, waits for them, and re-layouts  8.16 us

profile of v1, /device:TPU:1, one launch (start us, length us, event | category | flops | bytes accessed | tf_op | source)
XLA Modules:
  0.0 79.2 jit_solution(11634943581928616853)
XLA Ops:
  1.3 0.0 copy-start
  1.3 1.7 %copy-done = bf16[2560,512]{1,0:T(8,128)(2,1)S(1)} copy-done((bf16[2560,512]{1,0:T(8,128)(2,1)S(1)}, bf16[2560,512]{1,0:T(8,128)(2,1)}, u32[]{:S(2)}) %copy-start) | copy-done | bytes 2621464
  3.0 0.0 copy-start.1
  3.0 1.2 %copy-done.1 = f32[96,2560]{1,0:T(8,128)S(1)} copy-done((f32[96,2560]{1,0:T(8,128)S(1)}, f32[96,2560]{1,0:T(8,128)}, u32[]{:S(2)}) %copy-start.1) | copy-done | bytes 983064
  4.2 0.0 copy-start.2
  4.2 1.0 %copy-done.2 = bf16[96,2560]{1,0:T(8,128)(2,1)S(1)} copy-done((bf16[96,2560]{1,0:T(8,128)(2,1)S(1)}, bf16[96,2560]{1,0:T(8,128)(2,1)}, u32[]{:S(2)}) %copy-start.2) | copy-done | bytes 491544
  5.3 0.0 copy-start.3
  5.3 0.9 %copy-done.3 = bf16[10,3,2560]{2,1,0:T(4,128)(2,1)S(1)} copy-done((bf16[10,3,2560]{2,1,0:T(4,128)(2,1)S(1)}, bf16[10,3,2560]{2,1,0:T(4,128)(2,1)}, u32[]{:S(2)}) %copy-start.3) | copy-done | bytes 153624
  6.2 0.0 copy-start.4
  6.2 0.9 %copy-done.4 = s32[24576]{0:T(1024)S(1)} copy-done((s32[24576]{0:T(1024)S(1)}, s32[24576]{0:T(1024)}, u32[]{:S(2)}) %copy-start.4) | copy-done | bytes 98328
  7.1 0.0 copy-start.5
  7.1 0.7 copy-done.5
  7.7 69.7 %step.1 = (f32[96,2560]{1,0:T(8,128)S(1)}, bf16[96,2560]{1,0:T(8,128)(2,1)S(1)}) custom-call(f32[96,2560]{1,0:T(8,128)S(1)} %copy-done.1, bf16[96,2560]{1,0:T(8,128)(2,1)S(1)} %copy-done.2, bf16[10,3,2560]{2,1,0:T(4,128)(2,1)S(1)} %copy-done.3, s32[1]{0:T(128)S(6)} %copy.14.step_ref, f32[11]{0:T(128)S(1)} %copy-done.5, s32[192,128]{1,0:T(8,128)S(1)} %bitcast.1, ...), custom_call_target="tpu_custom_call" | custom-call | tf_op jit(solution)/shard_map/step/pallas_call | solution.py:348
  77.5 0.9 %copy.15 = f32[96,2560]{1,0:T(8,128)} copy(f32[96,2560]{1,0:T(8,128)S(1)} %get-tuple-element.4) | data formatting | bytes 1966080
  78.4 0.8 copy.16
Async XLA Ops:
  1.3 1.7 %copy-start = (bf16[2560,512]{1,0:T(8,128)(2,1)S(1)}, bf16[2560,512]{1,0:T(8,128)(2,1)}, u32[]{:S(2)}) copy-start(bf16[2560,512]{1,0:T(8,128)(2,1)} %wq_h.1) | copy-start | bytes 7864324
  3.0 1.2 %copy-start.1 = (f32[96,2560]{1,0:T(8,128)S(1)}, f32[96,2560]{1,0:T(8,128)}, u32[]{:S(2)}) copy-start(f32[96,2560]{1,0:T(8,128)} %state_h.1) | copy-start | bytes 2949124
  4.2 1.0 %copy-start.2 = (bf16[96,2560]{1,0:T(8,128)(2,1)S(1)}, bf16[96,2560]{1,0:T(8,128)(2,1)}, u32[]{:S(2)}) copy-start(bf16[96,2560]{1,0:T(8,128)(2,1)} %noise_h.1) | copy-start | bytes 1474564
  5.3 0.9 %copy-start.3 = (bf16[10,3,2560]{2,1,0:T(4,128)(2,1)S(1)}, bf16[10,3,2560]{2,1,0:T(4,128)(2,1)}, u32[]{:S(2)}) copy-start(bf16[10,3,2560]{2,1,0:T(4,128)(2,1)} %mod_ref.1) | copy-start | bytes 460804
  6.2 0.9 %copy-start.4 = (s32[24576]{0:T(1024)S(1)}, s32[24576]{0:T(1024)}, u32[]{:S(2)}) copy-start(s32[24576]{0:T(1024)} %param.15) | copy-start | bytes 294916
  7.1 0.7 copy-start.5

commit v2 on v0

v2 whole, which is shorter than its diff:
```python
import functools

import jax
import jax.numpy as jnp
from jax import lax
from jax.experimental import pallas as pl
from jax.experimental.pallas import tpu as pltpu
from jax.sharding import PartitionSpec as P

MESH = pl.DeviceIdType.MESH
ROWS = 96
HALF = 48
BF16 = jnp.bfloat16
F32 = jnp.float32


def kernel(
    state_h, noise_h, mod_h, step_ref, plan_ref, frame_h, wq_h, wk_h, wv_h, wo_h,
    adv_ref, est_ref,
    state, noise, modulation, frames, blocks, w_in, w_out, queries, kv, bias, mixed, mixed_sib,
    own_sum, far_sum, far_in, next_in, moved, moved_in, pace, pace_in,
    load_sem, send_sem, recv_sem, pair_send, pair_recv,
    far_send, far_recv, next_send, next_recv, extra_send, move_send, move_recv,
):
    width = state.shape[1]
    inner = w_out.shape[1]
    chunks, _, span = own_sum.shape
    slot = lax.axis_index("queue")
    shard = lax.axis_index("shard")
    side = lax.div(shard, 2)
    core = lax.rem(shard, 2)
    other = 1 - core
    last = 2 * lax.axis_size("queue") - 1
    chip = 2 * slot + side

    def at(step, which):
        there = chip + step
        return (lax.div(there, 2), 2 * lax.rem(there, 2) + which)

    sibling = (slot, 2 * side + other)
    has_behind = chip > 0
    has_ahead = chip < last
    low_extra = chip == 1
    high_extra = chip == last - 1

    barrier = pltpu.get_barrier_semaphore()

    def greet(condition, device):
        @pl.when(condition)
        def _():
            pl.semaphore_signal(barrier, inc=1, device_id=device, device_id_type=MESH)

    pl.semaphore_signal(barrier, inc=1, device_id=sibling, device_id_type=MESH)
    greet(has_behind, at(-1, core))
    greet(has_ahead, at(1, core))
    greet(chip >= 2, at(-2, core))
    greet((core == 0) & has_behind, at(-1, 1))
    greet((core == 0) & (chip == 0), at(1, 1))
    greet((core == 0) & (chip >= 3), at(-3, 0))
    greet((core == 0) & (chip >= 3), at(-3, 1))
    greet((core == 1) & has_ahead, at(1, 0))
    greet((core == 1) & (chip >= 2), at(-1, 0))

    def count(condition):
        return jnp.where(condition, 1, 0)

    greeted = (
        1 + count(has_ahead) + count(has_behind)
        + count((core == 0) & has_behind) + count((core == 0) & has_behind & has_ahead)
        + count((core == 1) & has_ahead) + count((core == 1) & low_extra)
        + count(chip <= last - 2) + count(chip <= last - 3)
    )

    def load(source, target, n):
        copy = pltpu.make_async_copy(source, target, load_sem.at[n])
        copy.start()
        return copy

    load_state = [
        load(state_h.at[pl.ds(k * HALF, HALF)], state.at[pl.ds(k * HALF, HALF)], k) for k in range(2)
    ]
    load_mod = load(mod_h, modulation, 2)
    load_frames = load(frame_h, frames, 3)

    level = step_ref[0]
    sigma_now = plan_ref[level]
    sigma_step = plan_ref[level + 1] - sigma_now
    load_mod.wait()
    modulate = modulation[level].astype(F32)
    shift, gain, gate = modulate[0:1], 1.0 + modulate[1:2], modulate[2:3]
    for n in range(ROWS // 16):
        if n % 3 == 0:
            load_state[n // 3].wait()
        rows = pl.ds(n * 16, 16)
        x = state[rows, :]
        x = x - jnp.mean(x, axis=-1, keepdims=True)
        spread = jnp.mean(jnp.square(x), axis=-1, keepdims=True)
        blocks[4 + core, rows, :] = (x * lax.rsqrt(spread + 1e-06) * gain + shift).astype(BF16)
    pl.semaphore_wait(barrier, greeted)

    def send(place, half, to_place, device, n):
        rows = pl.ds(half * HALF, HALF)
        return pltpu.make_async_remote_copy(
            src_ref=blocks.at[place, rows],
            dst_ref=blocks.at[to_place, rows],
            send_sem=send_sem.at[n],
            recv_sem=recv_sem.at[to_place, half],
            device_id=device,
            device_id_type=MESH,
        )

    def wait_block(place, half):
        here = blocks.at[place, pl.ds(half * HALF, HALF)]
        pltpu.make_async_copy(here, here, recv_sem.at[place, half]).wait()

    to_ahead = [send(4 + core, half, 2 + core, at(1, core), half) for half in range(2)]
    to_behind = [send(4 + core, half, 6 + core, at(-1, core), 2 + half) for half in range(2)]
    to_sibling = [send(4 + core, half, 4 + core, sibling, 4 + half) for half in range(2)]
    for half in range(2):
        pl.when(has_ahead)(to_ahead[half].start)
        pl.when(has_behind)(to_behind[half].start)
        to_sibling[half].start()
    load_w = [
        load(w, w_in.at[:, pl.ds(n * inner, inner)], 4 + n)
        for n, w in enumerate((wq_h, wk_h, wv_h))
    ]

    pace[...] = sigma_step * gate
    send_pace = pltpu.make_async_remote_copy(
        src_ref=pace, dst_ref=pace_in, send_sem=pair_send.at[4], recv_sem=pair_recv.at[4],
        device_id=at(2, core), device_id_type=MESH,
    )
    pl.when(chip <= last - 2)(send_pace.start)

    load_frames.wait()
    lines_all = (last + 1) * 192 // 128
    first = 192 * chip - 288 + (last + 1) * 192
    row = lax.div(first, 128)
    line = jnp.concatenate(
        [frames[pl.ds(lax.rem(row + n, lines_all), 1), :] for n in range(7)], axis=1
    ).astype(F32)
    line = jnp.broadcast_to(line, (8, 896))
    line = jnp.where(side == 0, pltpu.roll(line, 896 - 96, 1), pltpu.roll(line, 896 - 32, 1))
    column = jnp.broadcast_to(pltpu.roll(line, 896 - 96, 1)[0:1, :640], (128, 640)).T
    for n in range(4):
        keys = line if n == 0 else pltpu.roll(line, 896 - 96 * n, 1)
        gap = jnp.abs(column[(n + 1) * ROWS:(n + 2) * ROWS, 0:1] - keys[0:1, :512])
        bias[n] = jnp.where(gap <= 1.0, 0.0, -1e30)
    for condition, n, start in ((low_extra, 0, 0), (high_extra, 5, 3)):
        @pl.when(condition)
        def _():
            keys = line if start == 0 else pltpu.roll(line, 896 - 96 * start, 1)
            gap = jnp.abs(column[n * ROWS:(n + 1) * ROWS, 0:1] - keys[0:1, :512])
            bias[4] = jnp.where(gap <= 1.0, 0.0, -1e30)
    kv[pl.ds(8 * ROWS, 32), :] = jnp.zeros((32, 2 * inner), BF16)
    for condition, place in (
        (chip < 2, 1), (chip == 0, 2), (chip == 0, 3),
        (chip == last, 6), (chip == last, 7), (chip > last - 2, 0),
    ):
        @pl.when(condition)
        def _():
            blocks[place] = jnp.zeros((ROWS, width), BF16)

    def gather(parts):
        return jnp.concatenate([blocks[p, r:r + k] for p, r, k in parts], axis=0)

    def project_q(parts, into):
        for n in range(inner // 256):
            y = jnp.dot(gather(parts), w_in[:, n * 256:(n + 1) * 256], preferred_element_type=F32)
            y = y.astype(BF16) * 0.125
            done = 0
            for (_, _, k), r in zip(parts, into):
                queries[r:r + k, n * 256:(n + 1) * 256] = y[done:done + k]
                done += k

    def project_kv(parts, into):
        def part(n, _):
            cols = pl.ds(pl.multiple_of(n * 256, 256), 256)
            w = w_in[:, pl.ds(pl.multiple_of(inner + n * 256, 256), 256)]
            y = jnp.dot(gather(parts), w, preferred_element_type=F32).astype(BF16)
            done = 0
            for (_, _, k), r in zip(parts, into):
                kv[r:r + k, cols] = y[done:done + k]
                done += k
            return 0
        lax.fori_loop(0, 2 * inner // 256, part, 0)

    low = lax.broadcasted_iota(jnp.int32, (ROWS, 128), 1) < 64

    def attend(n, start):
        for g in range(inner // 128):
            q = queries[n * ROWS:(n + 1) * ROWS, g * 128:(g + 1) * 128]
            zero = jnp.zeros_like(q)
            q = jnp.concatenate([jnp.where(low, q, zero), jnp.where(low, zero, q)], axis=0)
            k = kv[start * ROWS:start * ROWS + 512, g * 128:(g + 1) * 128]
            v = kv[start * ROWS:start * ROWS + 512, inner + g * 128:inner + (g + 1) * 128]
            s = lax.dot_general(q, k, (((1,), (1,)), ((), ())), preferred_element_type=F32)
            s = s + jnp.concatenate([bias[n], bias[n]], axis=0)
            w = jnp.exp(s - jnp.max(s, axis=-1, keepdims=True))
            total = jnp.sum(w, axis=-1, keepdims=True)
            o = jnp.dot(w.astype(BF16), v, preferred_element_type=F32) / total
            mixed[n, :, g * 128:(g + 1) * 128] = jnp.where(low, o[:ROWS], o[ROWS:]).astype(BF16)

    for half in range(2):
        wait_block(4 + other, half)
    for copy in load_w:
        copy.wait()
    load_wo = load(wo_h, w_out.at[0], 7)
    load_noise = load(noise_h, noise, 8)
    share_w = pltpu.make_async_remote_copy(
        src_ref=wo_h, dst_ref=w_out.at[1], send_sem=pair_send.at[0], recv_sem=pair_recv.at[0],
        device_id=sibling, device_id_type=MESH,
    )
    share_w.start()
    project_q([(4, 0, 96), (5, 0, 96)], (ROWS, 2 * ROWS))
    project_kv([(4, 0, 96), (5, 0, 96)], (3 * ROWS, 4 * ROWS))

    core_rows = pl.ds(pl.multiple_of(core * HALF, 16), HALF)
    other_rows = pl.ds(pl.multiple_of(other * HALF, 16), HALF)
    both = has_behind & has_ahead

    def forward(place, half, n):
        wait_block(place, half)
        send(place, half, place, sibling, n).start()

    def relay(place, to_place, device, n):
        return pltpu.make_async_remote_copy(
            src_ref=blocks.at[place, core_rows], dst_ref=blocks.at[to_place, core_rows],
            send_sem=send_sem.at[n], recv_sem=recv_sem.at[to_place, core],
            device_id=device, device_id_type=MESH,
        )

    relay_ahead = relay(3, 1, at(1, core), 10)
    relay_behind = relay(6, 0, at(-1, core), 11)

    def when(condition, *steps):
        @pl.when(condition)
        def _():
            for step in steps:
                step()

    def neighbours(half):
        first_core, second_core = core == 0, core == 1
        when(first_core & has_behind, lambda: forward(2, half, 6 + half))
        when(first_core & has_ahead, lambda: forward(6, half, 8 + half))
        when(second_core & has_behind, lambda: forward(3, half, 6 + half))
        if half == 1:
            when(second_core & both, relay_ahead.start)
        else:
            when(first_core & both, relay_behind.start)
        when(second_core & has_ahead, lambda: forward(7, half, 8 + half))
        when(first_core & has_behind, lambda: wait_block(3, half))
        if half == 0:
            when(first_core & both, relay_ahead.start)
        when(first_core & has_ahead, lambda: wait_block(7, half))
        when(second_core & has_ahead, lambda: wait_block(6, half))
        if half == 1:
            when(second_core & both, relay_behind.start)
        when(second_core & has_behind, lambda: wait_block(2, half))
        r = half * HALF
        project_q([(3, r, HALF), (6, r, HALF)], (r, 3 * ROWS + r))
        project_kv(
            [(2, r, HALF), (3, r, HALF), (6, r, HALF), (7, r, HALF)],
            (ROWS + r, 2 * ROWS + r, 5 * ROWS + r, 6 * ROWS + r),
        )

    neighbours(0)
    neighbours(1)
    attend(1, 1)
    attend(2, 2)

    def swap(source, start, rows, n):
        return pltpu.make_async_remote_copy(
            src_ref=source, dst_ref=mixed_sib.at[pl.ds(start, rows)],
            send_sem=pair_send.at[n], recv_sem=pair_recv.at[n],
            device_id=sibling, device_id_type=MESH,
        )

    swap_own = swap(mixed.at[1 + other], ROWS, ROWS, 1)
    swap_own.start()

    def forward_far(k):
        here = blocks.at[k, core_rows]
        pltpu.make_async_copy(here, here, recv_sem.at[k, core]).wait()
        pltpu.make_async_remote_copy(
            src_ref=here, dst_ref=here, send_sem=send_sem.at[12 + k],
            recv_sem=recv_sem.at[k, core], device_id=sibling, device_id_type=MESH,
        ).start()

    def wait_far(k):
        here = blocks.at[k, other_rows]
        pltpu.make_async_copy(here, here, recv_sem.at[k, other]).wait()

    when(chip >= 2, lambda: forward_far(1))
    when(chip <= last - 2, lambda: forward_far(0))

    load_wo.wait()
    share_w.wait()
    swap_own.wait()
    moves = []
    for n in range(chunks):
        cols = slice(n * span, (n + 1) * span)
        y = jnp.dot(mixed[1 + core], w_out[0, :, cols], preferred_element_type=F32)
        y += jnp.dot(mixed_sib[ROWS:2 * ROWS], w_out[1, :, cols], preferred_element_type=F32)
        own_sum[n] = y
        moved[n] = (state[:, cols] + sigma_step * gate[:, cols] * y).astype(BF16)
        moves.append(pltpu.make_async_remote_copy(
            src_ref=moved.at[n], dst_ref=moved_in.at[n],
            send_sem=move_send.at[n], recv_sem=move_recv.at[n],
            device_id=at(2, core), device_id_type=MESH,
        ))
        pl.when(chip <= last - 2)(moves[n].start)

    def project_out(mine, theirs, n):
        cols = slice(n * span, (n + 1) * span)
        y = jnp.dot(mine, w_out[0, :, cols], preferred_element_type=F32)
        y += jnp.dot(theirs, w_out[1, :, cols], preferred_element_type=F32)
        return y.astype(BF16)

    def give(source, target, n, half, device, send, recv):
        return pltpu.make_async_remote_copy(
            src_ref=source, dst_ref=target.at[n, core_rows],
            send_sem=send, recv_sem=recv.at[n, core],
            device_id=device, device_id_type=MESH,
        )

    swap_extra = swap(mixed.at[4, other_rows], 2 * ROWS, HALF, 5)
    third = pl.ds(ROWS, HALF)

    def extra(n, device):
        return give(far_sum.at[n, third], far_in, n, 2, device, extra_send.at[n, 0], far_recv)

    def extra_next(n):
        return give(far_sum.at[n, third], next_in, n, 2, at(1, 0), extra_send.at[n, 1], next_recv)

    when(low_extra, lambda: project_q([(2, 0, ROWS)], (4 * ROWS,)), lambda: attend(4, 0))
    when(high_extra, lambda: project_q([(7, 0, ROWS)], (4 * ROWS,)), lambda: attend(4, 3))

    @pl.when(low_extra | high_extra)
    def _():
        swap_extra.start()
        swap_extra.wait()
        for n in range(chunks):
            far_sum[n, third] = project_out(mixed[4, core_rows], mixed_sib[2 * ROWS:2 * ROWS + HALF], n)
            when(low_extra, extra(n, at(-1, 0)).start, extra_next(n).start)
            when(high_extra, extra(n, at(1, 1)).start)

    when(chip >= 2, lambda: wait_far(1))
    when(chip <= last - 2, lambda: wait_far(0))
    project_kv([(0, 0, ROWS), (1, 0, ROWS)], (7 * ROWS, 0))
    attend(0, 0)
    swap_low = swap(mixed.at[0, other_rows], 0, HALF, 2)
    swap_low.start()
    attend(3, 3)
    swap_high = swap(mixed.at[3, other_rows], HALF, HALF, 3)
    swap_high.start()
    swap_low.wait()
    swap_high.wait()

    far = []
    far_mine = jnp.concatenate([mixed[0, core_rows, :], mixed[3, core_rows, :]], axis=0)
    for n in range(chunks):
        far_sum[n, 0:ROWS] = project_out(far_mine, mixed_sib[0:ROWS], n)
        below, above = far_sum.at[n, pl.ds(0, HALF)], far_sum.at[n, pl.ds(HALF, HALF)]
        group = (
            (has_behind, give(below, far_in, n, 0, at(-1, 1), far_send.at[n, 0], far_recv)),
            (has_ahead, give(above, far_in, n, 1, at(1, 0), far_send.at[n, 1], far_recv)),
            (both, give(below, next_in, n, 0, at(1, 1), next_send.at[n, 0], next_recv)),
            (chip <= last - 3, give(above, next_in, n, 1, at(3, 0), next_send.at[n, 1], next_recv)),
        )
        for condition, copy in group:
            pl.when(condition)(copy.start)
        far.extend(group)

    def wait_halves(target, n, sem):
        for k in range(2):
            here = target.at[n, pl.ds(k * HALF, HALF)]
            pltpu.make_async_copy(here, here, sem.at[n, k]).wait()

    load_noise.wait()

    @pl.when(slot == 0)
    def _():
        adv_ref[...] = noise[...].astype(F32)

    when(slot > 0, send_pace.wait_recv)
    for n in range(chunks):
        cols = slice(n * span, (n + 1) * span)
        wait_halves(far_in, n, far_recv)
        velocity = gate[:, cols] * (own_sum[n] + far_in[n].astype(F32))
        est_ref[:, cols] = (state[:, cols] - sigma_now * velocity).astype(BF16)

        @pl.when(slot > 0)
        def _():
            moves[n].wait_recv()
            wait_halves(next_in, n, next_recv)
            adv_ref[:, cols] = moved_in[n].astype(F32) + pace_in[:, cols] * next_in[n].astype(F32)

    def left(condition, n):
        here = blocks.at[0, pl.ds(0, HALF)]
        when(condition, lambda: pltpu.make_async_copy(here, here, send_sem.at[n]).wait())

    for half in range(2):
        left(has_ahead, half)
        left(has_behind, 2 + half)
        left(chip >= 0, 4 + half)
        left(has_behind, 6 + half)
        left(has_ahead, 8 + half)
    left(both, 10)
    left(both, 11)
    left(chip <= last - 2, 12)
    left(chip >= 2, 13)
    for condition, copy in far:
        when(condition, copy.wait_send)
    when(chip <= last - 2, send_pace.wait_send, *[copy.wait_send for copy in moves])
    for n in range(chunks):
        when(low_extra, extra(n, at(-1, 0)).wait_send, extra_next(n).wait_send)
        when(high_extra, extra(n, at(1, 1)).wait_send)


def on_device(state, noise, modulation, timesteps, plan, frame_ids, w_query, w_key, w_value, w_out):
    rows, width = state.shape
    inner = w_query.shape[1]
    span = 512
    chunks = width // span
    hbm = pl.BlockSpec(memory_space=pltpu.HBM)
    vmem = pl.BlockSpec(memory_space=pltpu.VMEM)
    smem = pl.BlockSpec(memory_space=pltpu.SMEM)
    dma = pltpu.SemaphoreType.DMA
    advanced, estimate = pl.pallas_call(
        kernel,
        out_shape=(
            jax.ShapeDtypeStruct((rows, width), F32),
            jax.ShapeDtypeStruct((rows, width), BF16),
        ),
        in_specs=[hbm, hbm, hbm, smem, smem, hbm, hbm, hbm, hbm, hbm],
        out_specs=(vmem, vmem),
        scratch_shapes=[
            pltpu.VMEM((rows, width), F32),
            pltpu.VMEM((rows, width), BF16),
            pltpu.VMEM(modulation.shape, BF16),
            pltpu.VMEM((frame_ids.size // 128, 128), jnp.int32),
            pltpu.VMEM((8, rows, width), BF16),
            pltpu.VMEM((width, 3 * inner), BF16),
            pltpu.VMEM((2, inner, width), BF16),
            pltpu.VMEM((5 * rows, inner), BF16),
            pltpu.VMEM((8 * rows + 32, 2 * inner), BF16),
            pltpu.VMEM((5, rows, 512), F32),
            pltpu.VMEM((5, rows, inner), BF16),
            pltpu.VMEM((3 * rows, inner), BF16),
            pltpu.VMEM((chunks, rows, span), F32),
            pltpu.VMEM((chunks, rows + HALF, span), BF16),
            pltpu.VMEM((chunks, rows, span), BF16),
            pltpu.VMEM((chunks, rows, span), BF16),
            pltpu.VMEM((chunks, rows, span), BF16),
            pltpu.VMEM((chunks, rows, span), BF16),
            pltpu.VMEM((1, width), F32),
            pltpu.VMEM((1, width), F32),
            dma((9,)),
            dma((14,)),
            dma((8, 2)),
            dma((6,)),
            dma((6,)),
            dma((chunks, 2)),
            dma((chunks, 2)),
            dma((chunks, 2)),
            dma((chunks, 2)),
            dma((chunks, 2)),
            dma((chunks,)),
            dma((chunks,)),
        ],
        compiler_params=pltpu.CompilerParams(
            collective_id=0, has_side_effects=True, vmem_limit_bytes=62914560
        ),
        name="step",
    )(
        state, noise, modulation, timesteps, plan, frame_ids.reshape(-1, 128),
        w_query, w_key, w_value, w_out,
    )
    return advanced, estimate


def solution(mesh):
    return jax.shard_map(
        on_device,
        mesh=mesh,
        in_specs=(
            P(("queue", "shard"), None),
            P("shard", None),
            P(),
            P("queue"),
            P(),
            P(),
            P(None, "shard"),
            P(None, "shard"),
            P(None, "shard"),
            P("shard", None),
        ),
        out_specs=(P(("queue", "shard"), None), P(("queue", "shard"), None)),
        check_vma=False,
    )
```

time: 183 us -> 66.7 us (0.36)
  waiting for transfers between devices: 106 us -> 0 us
  Pallas kernels: 0 us -> 61.2 us
  matrix products: 22.8 us -> 0 us
  between operations: 16.3 us -> 1.29 us
  other arithmetic: 14.8 us -> 0 us
  starting transfers between devices: 12.7 us -> 0 us
  local copies, waits for them, and re-layouts: 9.18 us -> 4.05 us
    pallas_call x0 -> x1, Pallas kernels: none -> 61.2 us  [on_device(): pl.pallas_call(kernel, out_shape=(jax.ShapeDtypeStruct((rows, width), F32...]
    ppermute x3 -> x0, waiting for transfers between devices: 42.3 us -> none  [the longest x1 26.1 us: extended(): lax.ppermute(lax.slice_in_dim(block, 0, width, axis=dim), axis, backward)]
    all_gather x1 -> x0, waiting for transfers between devices: 32.5 us -> none  [on_device(): shard_rows = lax.all_gather(normed, 'shard', axis=0, tiled=True)]
    reduce_scatter x1 -> x0, waiting for transfers between devices: 31.5 us -> none  [on_device(): lax.psum_scatter(jnp.dot(attended, w_out, preferred_element_type=jnp.floa...]
    dot_general x5 -> x0, matrix products: 16.8 us -> none  [the longest x1 7.53 us: one_block(): jnp.einsum('hqk,khd->qhd', weights, value_heads, preferred_element_type=j...]
    ppermute x3 -> x0, starting transfers between devices: 12.6 us -> none  [the longest x1 6.37 us: extended(): lax.ppermute(lax.slice_in_dim(block, 0, width, axis=dim), axis, backward)]
    slice x3 -> x0, local copies, waits for them, and re-layouts: 6.38 us -> none  [the longest x2 4.01 us: attend(): key_heads = key_values[:, 0].reshape(-1, head_count, HEAD_DIM)]
    convert_element_type x3 -> x0, other arithmetic: 6.06 us -> none  [the longest x1 3.11 us: on_device(): estimate = (state - sigma_now * velocity).astype(jnp.bfloat16)]
  transfers between devices with their start and end apart: 5 -> 0, of which waited for: 5 -> 0; matrix products, arithmetic and copies ran while one was open for 3% -> 0% of each run, Pallas kernels for 0% -> 0%
where the time goes in v2:
time: 66.7 us; the launch traced here: 66.5 us
  Pallas kernels  61.2 us (92%)
  local copies, waits for them, and re-layouts  4.05 us (6%)
  between operations  1.29 us (2%)
    pallas_call x1, Pallas kernels, on_device(): pl.pallas_call(kernel, out_shape=(jax.ShapeDtypeStruct((rows, width), F32...  61.2 us
    unnamed x2, local copies, waits for them, and re-layouts  4.05 us

profile of v2, /device:TPU:129, one launch (start us, length us, event | category | flops | bytes accessed | tf_op | source)
XLA Modules:
  0.0 66.5 jit_solution(14609249509139214627)
XLA Ops:
  1.3 61.2 %step.1 = (f32[96,2560]{1,0:T(8,128)}, bf16[96,2560]{1,0:T(8,128)(2,1)}) custom-call(f32[96,2560]{1,0:T(8,128)} %state_h.1, bf16[96,2560]{1,0:T(8,128)(2,1)} %noise_h.1, bf16[10,3,2560]{2,1,0:T(4,128)(2,1)} %mod_h.1, s32[1]{0:T(128)S(6)} %copy.14.step_ref, f32[11]{0:T(128)} %plan_ref.1, s32[192,128]{1,0:T(8,128)} %bitcast.1, bf16[2560,512]{1,0:T(8,128)(2,1)} %wq_h.1, ...), custom_call_target="tpu_custom_call" | custom-call | tf_op jit(solution)/shard_map/step/pallas_call | solution.py:430
  62.4 2.2 %copy.15 = f32[96,2560]{1,0:T(8,128)} copy(f32[96,2560]{1,0:T(8,128)} %get-tuple-element.4) | data formatting | bytes 1966080
  64.7 1.8 %copy.16 = bf16[96,2560]{1,0:T(8,128)(2,1)} copy(bf16[96,2560]{1,0:T(8,128)(2,1)} %get-tuple-element.5) | data formatting | bytes 983040

commit v3 on v2

--- a/solution.py
+++ b/solution.py
@@ -18,9 +18,9 @@
     state_h, noise_h, mod_h, step_ref, plan_ref, frame_h, wq_h, wk_h, wv_h, wo_h,
     adv_ref, est_ref,
     state, noise, modulation, frames, blocks, w_in, w_out, queries, kv, bias, mixed, mixed_sib,
-    own_sum, far_sum, far_in, next_in, moved, moved_in, pace, pace_in,
+    own_sum, far_sum, far_in, next_out, next_in, passing, moved, moved_in, pace,
     load_sem, send_sem, recv_sem, pair_send, pair_recv,
-    far_send, far_recv, next_send, next_recv, extra_send, move_send, move_recv,
+    far_send, far_recv, next_send, next_recv, extra_send, move_send, move_recv, pace_send, pace_recv, pass_send, pass_recv,
 ):
     width = state.shape[1]
     inner = w_out.shape[1]
@@ -38,6 +38,9 @@
         return (lax.div(there, 2), 2 * lax.rem(there, 2) + which)
 
     sibling = (slot, 2 * side + other)
+    turn = lax.rem(chip, 4)
+    detour = (turn == 3) & (chip <= last - 3)
+    relays = (turn == 2) & (chip <= last - 4)
     has_behind = chip > 0
     has_ahead = chip < last
     low_extra = chip == 1
@@ -53,22 +56,21 @@
     pl.semaphore_signal(barrier, inc=1, device_id=sibling, device_id_type=MESH)
     greet(has_behind, at(-1, core))
     greet(has_ahead, at(1, core))
-    greet(chip >= 2, at(-2, core))
     greet((core == 0) & has_behind, at(-1, 1))
     greet((core == 0) & (chip == 0), at(1, 1))
-    greet((core == 0) & (chip >= 3), at(-3, 0))
-    greet((core == 0) & (chip >= 3), at(-3, 1))
+    for k in range(2):
+        greet((core == 0) & (chip >= 3), at(jnp.where(turn == 2, -4, -3), k))
     greet((core == 1) & has_ahead, at(1, 0))
-    greet((core == 1) & (chip >= 2), at(-1, 0))
+    greet((core == 1) & has_behind, at(-1, 0))
 
     def count(condition):
         return jnp.where(condition, 1, 0)
 
     greeted = (
         1 + count(has_ahead) + count(has_behind)
-        + count((core == 0) & has_behind) + count((core == 0) & has_behind & has_ahead)
+        + count((core == 0) & has_behind) + count((core == 0) & has_ahead)
         + count((core == 1) & has_ahead) + count((core == 1) & low_extra)
-        + count(chip <= last - 2) + count(chip <= last - 3)
+        + count((chip <= last - 3) & (turn != 3)) + count(relays)
     )
 
     def load(source, target, n):
@@ -125,12 +127,20 @@
         for n, w in enumerate((wq_h, wk_h, wv_h))
     ]
 
-    pace[...] = sigma_step * gate
-    send_pace = pltpu.make_async_remote_copy(
-        src_ref=pace, dst_ref=pace_in, send_sem=pair_send.at[4], recv_sem=pair_recv.at[4],
-        device_id=at(2, core), device_id_type=MESH,
-    )
-    pl.when(chip <= last - 2)(send_pace.start)
+    pace[0] = sigma_step * gate
+    step = 2 * core - 1
+    paces = [
+        pltpu.make_async_remote_copy(
+            src_ref=pace.at[0], dst_ref=pace.at[2 - core],
+            send_sem=pace_send.at[k], recv_sem=pace_recv.at[1 - core],
+            device_id=at(step, k), device_id_type=MESH,
+        )
+        for k in range(2)
+    ]
+    gives = chip <= last - 2
+    gives_pace = gives & ((core == 1) | has_behind)
+    for copy in paces:
+        pl.when(gives_pace)(copy.start)
 
     load_frames.wait()
     lines_all = (last + 1) * 192 // 128
@@ -298,24 +308,34 @@
     share_w.wait()
     swap_own.wait()
     moves = []
+    low_end = (chip == 0) & (core == 0)
+    which = jnp.where(low_end, 2, 1 - core)
+    place = pl.multiple_of(which * HALF, 16)
     for n in range(chunks):
         cols = slice(n * span, (n + 1) * span)
         y = jnp.dot(mixed[1 + core], w_out[0, :, cols], preferred_element_type=F32)
         y += jnp.dot(mixed_sib[ROWS:2 * ROWS], w_out[1, :, cols], preferred_element_type=F32)
         own_sum[n] = y
-        moved[n] = (state[:, cols] + sigma_step * gate[:, cols] * y).astype(BF16)
-        moves.append(pltpu.make_async_remote_copy(
-            src_ref=moved.at[n], dst_ref=moved_in.at[n],
-            send_sem=move_send.at[n], recv_sem=move_recv.at[n],
-            device_id=at(2, core), device_id_type=MESH,
-        ))
-        pl.when(chip <= last - 2)(moves[n].start)
+        moved[n] = (state[:, cols] + pace[0, :, cols] * y).astype(BF16)
+        for k in range(2):
+            copy = pltpu.make_async_remote_copy(
+                src_ref=moved.at[n, pl.ds(k * HALF, HALF)], dst_ref=moved_in.at[n, pl.ds(place, HALF)],
+                send_sem=move_send.at[n, k],
+                recv_sem=move_recv.at[n, which],
+                device_id=at(jnp.where(low_end, 1, step), k), device_id_type=MESH,
+            )
+            pl.when(gives)(copy.start)
+            moves.append(copy)
+
+    def wait_moved(condition, n, k):
+        here = moved_in.at[n, pl.ds(k * HALF, HALF)]
+        when(condition, lambda: pltpu.make_async_copy(here, here, move_recv.at[n, k]).wait())
 
     def project_out(mine, theirs, n):
         cols = slice(n * span, (n + 1) * span)
         y = jnp.dot(mine, w_out[0, :, cols], preferred_element_type=F32)
         y += jnp.dot(theirs, w_out[1, :, cols], preferred_element_type=F32)
-        return y.astype(BF16)
+        return y
 
     def give(source, target, n, half, device, send, recv):
         return pltpu.make_async_remote_copy(
@@ -331,20 +351,12 @@
         return give(far_sum.at[n, third], far_in, n, 2, device, extra_send.at[n, 0], far_recv)
 
     def extra_next(n):
-        return give(far_sum.at[n, third], next_in, n, 2, at(1, 0), extra_send.at[n, 1], next_recv)
+        return give(next_out.at[n, third], next_in, n, 2, at(1, 0), extra_send.at[n, 1], next_recv)
 
     when(low_extra, lambda: project_q([(2, 0, ROWS)], (4 * ROWS,)), lambda: attend(4, 0))
     when(high_extra, lambda: project_q([(7, 0, ROWS)], (4 * ROWS,)), lambda: attend(4, 3))
 
-    @pl.when(low_extra | high_extra)
-    def _():
-        swap_extra.start()
-        swap_extra.wait()
-        for n in range(chunks):
-            far_sum[n, third] = project_out(mixed[4, core_rows], mixed_sib[2 * ROWS:2 * ROWS + HALF], n)
-            when(low_extra, extra(n, at(-1, 0)).start, extra_next(n).start)
-            when(high_extra, extra(n, at(1, 1)).start)
-
+    when(low_extra | high_extra, swap_extra.start)
     when(chip >= 2, lambda: wait_far(1))
     when(chip <= last - 2, lambda: wait_far(0))
     project_kv([(0, 0, ROWS), (1, 0, ROWS)], (7 * ROWS, 0))
@@ -357,33 +369,69 @@
     swap_low.wait()
     swap_high.wait()
 
+    for condition, k in ((both, 0), (chip <= last - 3, 1)):
+        here = pace.at[1 + k]
+        when(condition, pltpu.make_async_copy(here, here, pace_recv.at[k]).wait)
     far = []
     far_mine = jnp.concatenate([mixed[0, core_rows, :], mixed[3, core_rows, :]], axis=0)
     for n in range(chunks):
-        far_sum[n, 0:ROWS] = project_out(far_mine, mixed_sib[0:ROWS], n)
+        cols = slice(n * span, (n + 1) * span)
+        y = project_out(far_mine, mixed_sib[0:ROWS], n)
+        far_sum[n, 0:ROWS] = y.astype(BF16)
+        wait_moved(both, n, 0)
+        wait_moved(chip <= last - 3, n, 1)
+        for k in range(2):
+            rows = pl.ds(k * HALF, HALF)
+            base = moved_in[n, rows].astype(F32)
+            next_out[n, rows] = (base + pace[1 + k, :, cols] * y[k * HALF:(k + 1) * HALF]).astype(BF16)
         below, above = far_sum.at[n, pl.ds(0, HALF)], far_sum.at[n, pl.ds(HALF, HALF)]
+        next_below, next_above = next_out.at[n, pl.ds(0, HALF)], next_out.at[n, pl.ds(HALF, HALF)]
         group = (
             (has_behind, give(below, far_in, n, 0, at(-1, 1), far_send.at[n, 0], far_recv)),
             (has_ahead, give(above, far_in, n, 1, at(1, 0), far_send.at[n, 1], far_recv)),
-            (both, give(below, next_in, n, 0, at(1, 1), next_send.at[n, 0], next_recv)),
-            (chip <= last - 3, give(above, next_in, n, 1, at(3, 0), next_send.at[n, 1], next_recv)),
+            (both, give(next_below, next_in, n, 0, at(1, 1), next_send.at[n, 0], next_recv)),
+            ((chip <= last - 3) & (turn != 3), give(next_above, next_in, n, 1, at(3, 0), next_send.at[n, 1], next_recv)),
+            (detour, pltpu.make_async_remote_copy(
+                src_ref=next_above, dst_ref=passing.at[n], send_sem=next_send.at[n, 1],
+                recv_sem=pass_recv.at[n], device_id=at(-1, core), device_id_type=MESH,
+            )),
         )
         for condition, copy in group:
             pl.when(condition)(copy.start)
         far.extend(group)
+
+    @pl.when(low_extra | high_extra)
+    def _():
+        swap_extra.wait()
+        for n in range(chunks):
+            cols = slice(n * span, (n + 1) * span)
+            y = project_out(mixed[4, core_rows], mixed_sib[2 * ROWS:2 * ROWS + HALF], n)
+            far_sum[n, third] = y.astype(BF16)
+            wait_moved(low_extra, n, 2)
+            base = moved_in[n, third].astype(F32)
+            next_out[n, third] = (base + pace[0, :, cols] * y).astype(BF16)
+            when(low_extra, extra(n, at(-1, 0)).start, extra_next(n).start)
+            when(high_extra, extra(n, at(1, 1)).start)
 
     def wait_halves(target, n, sem):
         for k in range(2):
             here = target.at[n, pl.ds(k * HALF, HALF)]
             pltpu.make_async_copy(here, here, sem.at[n, k]).wait()
 
+    def onward(n):
+        return give(passing.at[n], next_in, n, 1, at(4, 0), pass_send.at[n], next_recv)
+
+    def pass_on(n):
+        pltpu.make_async_copy(passing.at[n], passing.at[n], pass_recv.at[n]).wait()
+        onward(n).start()
+
+    when(relays, *[functools.partial(pass_on, n) for n in range(chunks)])
     load_noise.wait()
 
     @pl.when(slot == 0)
     def _():
         adv_ref[...] = noise[...].astype(F32)
 
-    when(slot > 0, send_pace.wait_recv)
     for n in range(chunks):
         cols = slice(n * span, (n + 1) * span)
         wait_halves(far_in, n, far_recv)
@@ -392,9 +440,8 @@
 
         @pl.when(slot > 0)
         def _():
-            moves[n].wait_recv()
             wait_halves(next_in, n, next_recv)
-            adv_ref[:, cols] = moved_in[n].astype(F32) + pace_in[:, cols] * next_in[n].astype(F32)
+            adv_ref[:, cols] = next_in[n].astype(F32)
 
     def left(condition, n):
         here = blocks.at[0, pl.ds(0, HALF)]
@@ -412,10 +459,23 @@
     left(chip >= 2, 13)
     for condition, copy in far:
         when(condition, copy.wait_send)
-    when(chip <= last - 2, send_pace.wait_send, *[copy.wait_send for copy in moves])
+    for n in range(chunks):
+        when(relays, onward(n).wait_send)
+    when(gives_pace, *[copy.wait_send for copy in paces])
+    when(gives, *[copy.wait_send for copy in moves])
     for n in range(chunks):
         when(low_extra, extra(n, at(-1, 0)).wait_send, extra_next(n).wait_send)
         when(high_extra, extra(n, at(1, 1)).wait_send)
+
+
+def finish(adv_in, est_in, adv_out, est_out, sem):
+    copies = [
+        pltpu.make_async_copy(adv_in, adv_out, sem.at[0]), pltpu.make_async_copy(est_in, est_out, sem.at[1])
+    ]
+    for copy in copies:
+        copy.start()
+    for copy in copies:
+        copy.wait()
 
 
 def on_device(state, noise, modulation, timesteps, plan, frame_ids, w_query, w_key, w_value, w_out):
@@ -451,11 +511,12 @@
             pltpu.VMEM((chunks, rows, span), F32),
             pltpu.VMEM((chunks, rows + HALF, span), BF16),
             pltpu.VMEM((chunks, rows, span), BF16),
+            pltpu.VMEM((chunks, rows + HALF, span), BF16),
             pltpu.VMEM((chunks, rows, span), BF16),
+            pltpu.VMEM((chunks, HALF, span), BF16),
             pltpu.VMEM((chunks, rows, span), BF16),
-            pltpu.VMEM((chunks, rows, span), BF16),
-            pltpu.VMEM((1, width), F32),
-            pltpu.VMEM((1, width), F32),
+            pltpu.VMEM((chunks, rows + HALF, span), BF16),
+            pltpu.VMEM((3, 1, width), F32),
             dma((9,)),
             dma((14,)),
             dma((8, 2)),
@@ -466,6 +527,10 @@
             dma((chunks, 2)),
             dma((chunks, 2)),
             dma((chunks, 2)),
+            dma((chunks, 2)),
+            dma((chunks, 3)),
+            dma((2,)),
+            dma((2,)),
             dma((chunks,)),
             dma((chunks,)),
         ],
@@ -477,7 +542,17 @@
         state, noise, modulation, timesteps, plan, frame_ids.reshape(-1, 128),
         w_query, w_key, w_value, w_out,
     )
-    return advanced, estimate
+    return pl.pallas_call(
+        finish,
+        out_shape=(
+            jax.ShapeDtypeStruct((rows, width), F32),
+            jax.ShapeDtypeStruct((rows, width), BF16),
+        ),
+        in_specs=[vmem, vmem],
+        out_specs=(hbm, hbm),
+        scratch_shapes=[dma((2,))],
+        name="finish",
+    )(advanced, estimate)
 
 
 def solution(mesh):

time: 66.7 us -> 58.5 us (0.88); the launches traced: 66.5 us -> 57.4 us
  Pallas kernels: 61.2 us -> 56.1 us
  local copies, waits for them, and re-layouts: 4.05 us -> 0 us
    pallas_call x1, Pallas kernels: 61.2 us -> 53.7 us  [on_device(): pl.pallas_call(kernel, out_shape=(jax.ShapeDtypeStruct((rows, width), F32...]
    unnamed x2 -> x0, local copies, waits for them, and re-layouts: 4.05 us -> none
    pallas_call x0 -> x1, Pallas kernels: none -> 2.44 us  [on_device(): pl.pallas_call(finish, out_shape=(jax.ShapeDtypeStruct((rows, width), F32...]
where the time goes in v3:
time: 58.5 us; the launch traced here: 57.4 us
  Pallas kernels  56.1 us (96%)
  between operations  1.29 us (2%)
    pallas_call x1, Pallas kernels, on_device(): pl.pallas_call(kernel, out_shape=(jax.ShapeDtypeStruct((rows, width), F32...  53.7 us
    pallas_call x1, Pallas kernels, on_device(): pl.pallas_call(finish, out_shape=(jax.ShapeDtypeStruct((rows, width), F32...  2.44 us

profile of v3, /device:TPU:129, one launch (start us, length us, event | category | flops | bytes accessed | tf_op | source)
XLA Modules:
  0.0 57.4 jit_solution(7142777708688957886)
XLA Ops:
  1.3 53.7 %step.1 = (f32[96,2560]{1,0:T(8,128)}, bf16[96,2560]{1,0:T(8,128)(2,1)}) custom-call(f32[96,2560]{1,0:T(8,128)} %state_h.1, bf16[96,2560]{1,0:T(8,128)(2,1)} %noise_h.1, bf16[10,3,2560]{2,1,0:T(4,128)(2,1)} %mod_h.1, s32[1]{0:T(128)S(6)} %copy.12.step_ref, f32[11]{0:T(128)} %plan_ref.1, s32[192,128]{1,0:T(8,128)} %bitcast.1, bf16[2560,512]{1,0:T(8,128)(2,1)} %wq_h.1, ...), custom_call_target="tpu_custom_call" | custom-call | tf_op jit(solution)/shard_map/step/pallas_call | solution.py:490
  55.0 2.4 %finish.1 = (f32[96,2560]{1,0:T(8,128)}, bf16[96,2560]{1,0:T(8,128)(2,1)}) custom-call(f32[96,2560]{1,0:T(8,128)} %get-tuple-element.4.adv_in, bf16[96,2560]{1,0:T(8,128)(2,1)} %get-tuple-element.5.est_in), custom_call_target="tpu_custom_call" | custom-call | tf_op jit(solution)/shard_map/finish/pallas_call | solution.py:545

commit v4 on v3

--- a/solution.py
+++ b/solution.py
@@ -16,10 +16,10 @@
 
 def kernel(
     state_h, noise_h, mod_h, step_ref, plan_ref, frame_h, wq_h, wk_h, wv_h, wo_h,
-    adv_ref, est_ref,
-    state, noise, modulation, frames, blocks, w_in, w_out, queries, kv, bias, mixed, mixed_sib,
+    adv_h, est_h,
+    est, state, noise, modulation, frames, blocks, w_in, w_out, queries, kv, bias, mixed, mixed_sib,
     own_sum, far_sum, far_in, next_out, next_in, passing, moved, moved_in, pace,
-    load_sem, send_sem, recv_sem, pair_send, pair_recv,
+    store_sem, load_sem, send_sem, recv_sem, pair_send, pair_recv,
     far_send, far_recv, next_send, next_recv, extra_send, move_send, move_recv, pace_send, pace_recv, pass_send, pass_recv,
 ):
     width = state.shape[1]
@@ -90,16 +90,6 @@
     load_mod.wait()
     modulate = modulation[level].astype(F32)
     shift, gain, gate = modulate[0:1], 1.0 + modulate[1:2], modulate[2:3]
-    for n in range(ROWS // 16):
-        if n % 3 == 0:
-            load_state[n // 3].wait()
-        rows = pl.ds(n * 16, 16)
-        x = state[rows, :]
-        x = x - jnp.mean(x, axis=-1, keepdims=True)
-        spread = jnp.mean(jnp.square(x), axis=-1, keepdims=True)
-        blocks[4 + core, rows, :] = (x * lax.rsqrt(spread + 1e-06) * gain + shift).astype(BF16)
-    pl.semaphore_wait(barrier, greeted)
-
     def send(place, half, to_place, device, n):
         rows = pl.ds(half * HALF, HALF)
         return pltpu.make_async_remote_copy(
@@ -119,6 +109,15 @@
     to_behind = [send(4 + core, half, 6 + core, at(-1, core), 2 + half) for half in range(2)]
     to_sibling = [send(4 + core, half, 4 + core, sibling, 4 + half) for half in range(2)]
     for half in range(2):
+        load_state[half].wait()
+        for n in range(3 * half, 3 * half + 3):
+            rows = pl.ds(n * 16, 16)
+            x = state[rows, :]
+            x = x - jnp.mean(x, axis=-1, keepdims=True)
+            spread = jnp.mean(jnp.square(x), axis=-1, keepdims=True)
+            blocks[4 + core, rows, :] = (x * lax.rsqrt(spread + 1e-06) * gain + shift).astype(BF16)
+        if half == 0:
+            pl.semaphore_wait(barrier, greeted)
         pl.when(has_ahead)(to_ahead[half].start)
         pl.when(has_behind)(to_behind[half].start)
         to_sibling[half].start()
@@ -396,9 +395,12 @@
                 recv_sem=pass_recv.at[n], device_id=at(-1, core), device_id_type=MESH,
             )),
         )
-        for condition, copy in group:
+        for condition, copy in group[:0:-1]:
             pl.when(condition)(copy.start)
         far.extend(group)
+    for n in range(chunks):
+        condition, copy = far[5 * n]
+        pl.when(condition)(copy.start)
 
     @pl.when(low_extra | high_extra)
     def _():
@@ -428,20 +430,31 @@
     when(relays, *[functools.partial(pass_on, n) for n in range(chunks)])
     load_noise.wait()
 
-    @pl.when(slot == 0)
-    def _():
-        adv_ref[...] = noise[...].astype(F32)
-
+    def store(source, target, n):
+        return pltpu.make_async_copy(source, target, store_sem.at[n])
+
+    when(slot == 0, store(noise, adv_h, 0).start)
+    stores = []
     for n in range(chunks):
         cols = slice(n * span, (n + 1) * span)
         wait_halves(far_in, n, far_recv)
         velocity = gate[:, cols] * (own_sum[n] + far_in[n].astype(F32))
-        est_ref[:, cols] = (state[:, cols] - sigma_now * velocity).astype(BF16)
+        est[:, cols] = (state[:, cols] - sigma_now * velocity).astype(BF16)
 
         @pl.when(slot > 0)
         def _():
             wait_halves(next_in, n, next_recv)
-            adv_ref[:, cols] = next_in[n].astype(F32)
+            store(next_in.at[n], adv_h.at[:, pl.ds(n * span, span)], 1 + n).start()
+
+        here = pl.ds(n * span, span)
+        stores.append(store(est.at[:, here], est_h.at[:, here], 1 + chunks + n))
+        stores[-1].start()
+
+    for n in range(chunks):
+        when(slot > 0, store(next_in.at[n], adv_h.at[:, pl.ds(n * span, span)], 1 + n).wait)
+    when(slot == 0, store(noise, adv_h, 0).wait)
+    for copy in stores:
+        copy.wait()
 
     def left(condition, n):
         here = blocks.at[0, pl.ds(0, HALF)]
@@ -468,13 +481,22 @@
         when(high_extra, extra(n, at(1, 1)).wait_send)
 
 
-def finish(adv_in, est_in, adv_out, est_out, sem):
-    copies = [
-        pltpu.make_async_copy(adv_in, adv_out, sem.at[0]), pltpu.make_async_copy(est_in, est_out, sem.at[1])
-    ]
-    for copy in copies:
+def finish(adv_in, est_in, adv_out, est_out, adv_bf16, adv, est, sem):
+    size = ROWS // 2
+    rows = [pl.ds(k * size, size) for k in range(2)]
+    ins = [pltpu.make_async_copy(adv_in.at[r], adv_bf16.at[r], sem.at[k]) for k, r in enumerate(rows)]
+    ins.append(pltpu.make_async_copy(est_in, est, sem.at[2]))
+    outs = [pltpu.make_async_copy(adv.at[r], adv_out.at[r], sem.at[3 + k]) for k, r in enumerate(rows)]
+    outs.append(pltpu.make_async_copy(est, est_out, sem.at[5]))
+    for copy in ins:
         copy.start()
-    for copy in copies:
+    for k, r in enumerate(rows):
+        ins[k].wait()
+        adv[r, :] = adv_bf16[r, :].astype(F32)
+        outs[k].start()
+    ins[2].wait()
+    outs[2].start()
+    for copy in outs:
         copy.wait()
 
 
@@ -484,18 +506,18 @@
     span = 512
     chunks = width // span
     hbm = pl.BlockSpec(memory_space=pltpu.HBM)
-    vmem = pl.BlockSpec(memory_space=pltpu.VMEM)
     smem = pl.BlockSpec(memory_space=pltpu.SMEM)
     dma = pltpu.SemaphoreType.DMA
     advanced, estimate = pl.pallas_call(
         kernel,
         out_shape=(
-            jax.ShapeDtypeStruct((rows, width), F32),
+            jax.ShapeDtypeStruct((rows, width), BF16),
             jax.ShapeDtypeStruct((rows, width), BF16),
         ),
         in_specs=[hbm, hbm, hbm, smem, smem, hbm, hbm, hbm, hbm, hbm],
-        out_specs=(vmem, vmem),
+        out_specs=(hbm, hbm),
         scratch_shapes=[
+            pltpu.VMEM((rows, width), BF16),
             pltpu.VMEM((rows, width), F32),
             pltpu.VMEM((rows, width), BF16),
             pltpu.VMEM(modulation.shape, BF16),
@@ -517,6 +539,7 @@
             pltpu.VMEM((chunks, rows, span), BF16),
             pltpu.VMEM((chunks, rows + HALF, span), BF16),
             pltpu.VMEM((3, 1, width), F32),
+            dma((1 + 2 * chunks,)),
             dma((9,)),
             dma((14,)),
             dma((8, 2)),
@@ -548,9 +571,14 @@
             jax.ShapeDtypeStruct((rows, width), F32),
             jax.ShapeDtypeStruct((rows, width), BF16),
         ),
-        in_specs=[vmem, vmem],
+        in_specs=[hbm, hbm],
         out_specs=(hbm, hbm),
-        scratch_shapes=[dma((2,))],
+        scratch_shapes=[
+            pltpu.VMEM((rows, width), BF16),
+            pltpu.VMEM((rows, width), F32),
+            pltpu.VMEM((rows, width), BF16),
+            dma((6,)),
+        ],
         name="finish",
     )(advanced, estimate)
 

time: 58.5 us -> 56.9 us (0.973); the launches traced: 57.4 us -> 56.4 us
  Pallas kernels: 56.1 us -> 55.1 us
    pallas_call x1, Pallas kernels: 53.7 us -> 53 us  [on_device(): pl.pallas_call(kernel, out_shape=(jax.ShapeDtypeStruct((rows, width), BF1...]
where the time goes in v4:
time: 56.9 us; the launch traced here: 56.4 us
  Pallas kernels  55.1 us (97%)
  between operations  1.29 us (2%)
    pallas_call x1, Pallas kernels, on_device(): pl.pallas_call(kernel, out_shape=(jax.ShapeDtypeStruct((rows, width), BF1...  53 us
    pallas_call x1, Pallas kernels, on_device(): pl.pallas_call(finish, out_shape=(jax.ShapeDtypeStruct((rows, width), F32...  2.13 us

profile of v4, /device:TPU:129, one launch (start us, length us, event | category | flops | bytes accessed | tf_op | source)
XLA Modules:
  0.0 56.4 jit_solution(15162713245913032632)
XLA Ops:
  1.3 53.0 %step.1 = (bf16[96,2560]{1,0:T(8,128)(2,1)}, bf16[96,2560]{1,0:T(8,128)(2,1)}) custom-call(f32[96,2560]{1,0:T(8,128)} %state_h.1, bf16[96,2560]{1,0:T(8,128)(2,1)} %noise_h.1, bf16[10,3,2560]{2,1,0:T(4,128)(2,1)} %mod_h.1, s32[1]{0:T(128)S(6)} %copy.12.step_ref, f32[11]{0:T(128)} %plan_ref.1, s32[192,128]{1,0:T(8,128)} %bitcast.1, bf16[2560,512]{1,0:T(8,128)(2,1)} %wq_h.1, ...), custom_call_target="tpu_custom_call" | custom-call | tf_op jit(solution)/shard_map/step/pallas_call | solution.py:511
  54.3 2.1 %finish.1 = (f32[96,2560]{1,0:T(8,128)}, bf16[96,2560]{1,0:T(8,128)(2,1)}) custom-call(bf16[96,2560]{1,0:T(8,128)(2,1)} %get-tuple-element.4.adv_in, bf16[96,2560]{1,0:T(8,128)(2,1)} %get-tuple-element.5.est_in), custom_call_target="tpu_custom_call" | custom-call | tf_op jit(solution)/shard_map/finish/pallas_call | solution.py:568

commit v5 on v4

--- a/solution.py
+++ b/solution.py
@@ -482,20 +482,20 @@
 
 
 def finish(adv_in, est_in, adv_out, est_out, adv_bf16, adv, est, sem):
-    size = ROWS // 2
-    rows = [pl.ds(k * size, size) for k in range(2)]
+    size = ROWS // 3
+    rows = [pl.ds(k * size, size) for k in range(3)]
     ins = [pltpu.make_async_copy(adv_in.at[r], adv_bf16.at[r], sem.at[k]) for k, r in enumerate(rows)]
-    ins.append(pltpu.make_async_copy(est_in, est, sem.at[2]))
-    outs = [pltpu.make_async_copy(adv.at[r], adv_out.at[r], sem.at[3 + k]) for k, r in enumerate(rows)]
-    outs.append(pltpu.make_async_copy(est, est_out, sem.at[5]))
+    ins.append(pltpu.make_async_copy(est_in, est, sem.at[3]))
+    outs = [pltpu.make_async_copy(adv.at[r], adv_out.at[r], sem.at[4 + k]) for k, r in enumerate(rows)]
+    outs.append(pltpu.make_async_copy(est, est_out, sem.at[7]))
     for copy in ins:
         copy.start()
     for k, r in enumerate(rows):
         ins[k].wait()
         adv[r, :] = adv_bf16[r, :].astype(F32)
         outs[k].start()
-    ins[2].wait()
-    outs[2].start()
+    ins[3].wait()
+    outs[3].start()
     for copy in outs:
         copy.wait()
 
@@ -577,7 +577,7 @@
             pltpu.VMEM((rows, width), BF16),
             pltpu.VMEM((rows, width), F32),
             pltpu.VMEM((rows, width), BF16),
-            dma((6,)),
+            dma((8,)),
         ],
         name="finish",
     )(advanced, estimate)

time: 56.9 us -> 56.9 us (level)
  no operation moved by 1% of the time
where the time goes in v5:
time: 56.9 us; the launch traced here: 56.4 us
  Pallas kernels  55.1 us (97%)
  between operations  1.29 us (2%)
    pallas_call x1, Pallas kernels, on_device(): pl.pallas_call(kernel, out_shape=(jax.ShapeDtypeStruct((rows, width), BF1...  53 us
    pallas_call x1, Pallas kernels, on_device(): pl.pallas_call(finish, out_shape=(jax.ShapeDtypeStruct((rows, width), F32...  2.12 us

profile of v5, /device:TPU:129, one launch (start us, length us, event | category | flops | bytes accessed | tf_op | source)
XLA Modules:
  0.0 56.4 jit_solution(8394888876738178404)
XLA Ops:
  1.3 53.0 %step.1 = (bf16[96,2560]{1,0:T(8,128)(2,1)}, bf16[96,2560]{1,0:T(8,128)(2,1)}) custom-call(f32[96,2560]{1,0:T(8,128)} %state_h.1, bf16[96,2560]{1,0:T(8,128)(2,1)} %noise_h.1, bf16[10,3,2560]{2,1,0:T(4,128)(2,1)} %mod_h.1, s32[1]{0:T(128)S(6)} %copy.12.step_ref, f32[11]{0:T(128)} %plan_ref.1, s32[192,128]{1,0:T(8,128)} %bitcast.1, bf16[2560,512]{1,0:T(8,128)(2,1)} %wq_h.1, ...), custom_call_target="tpu_custom_call" | custom-call | tf_op jit(solution)/shard_map/step/pallas_call | solution.py:511
  54.3 2.1 %finish.1 = (f32[96,2560]{1,0:T(8,128)}, bf16[96,2560]{1,0:T(8,128)(2,1)}) custom-call(bf16[96,2560]{1,0:T(8,128)(2,1)} %get-tuple-element.4.adv_in, bf16[96,2560]{1,0:T(8,128)(2,1)} %get-tuple-element.5.est_in), custom_call_target="tpu_custom_call" | custom-call | tf_op jit(solution)/shard_map/finish/pallas_call | solution.py:568
